TPU v7x, 512 devices: a whole 4x4x16 slice. The times are simulated.
512 devices in a mesh: slab: 64 (over z, x_hi, core), col: 8 (over x_lo, y).
Axes of the slice: x: 4 (x_hi: 2, x_lo: 2; x = x_hi * 2 + x_lo), y: 4, z: 16, core: 2. Of those that a mesh axis runs over, the one named last changes fastest.
Arguments:
- positions: float32 [3, 4194304], P(None, ('slab', 'col')), may hold values from -3 to 3
- mass: float32 [4194304], P(('slab', 'col')), may hold values from 0.5 to 2
- smooth: float32 [4194304], P(('slab', 'col')), may hold values from 0.6 to 1.6
- cell_y: int32 [4194304], P(('slab', 'col')), may hold values from 0 to 127
- cell_z: int32 [4194304], P(('slab', 'col')), may hold values from 0 to 1023
- cic_frac: float32 [3, 4194304], P(None, ('slab', 'col')), may hold values from 0 to 1
- pair_blocks: int32 [32768, 9], P(('slab', 'col')), may hold values from 0 to 127, as said below
- pair_count: int32 [32768], P(('slab', 'col')), may hold values from 3 to 9, as said below
Outputs:
- density: float32 [4194304], P(('slab', 'col'))
- acceleration: float32 [3, 4194304], P(None, ('slab', 'col'))
- mesh_mass: float32 [128, 1024, 1024], P('slab', 'col')
Inputs may be any that keep to these rules, and one draw needn't show every extreme that they name: `pair_blocks`: slot 0 of block b names b itself (index 32 + b mod 64), slot 1 the block 32 before it and slot 2 the block 32 after it; every entry lies within 32 blocks of the block itself, live entries of a row are distinct, dead slots repeat slot 0. `pair_count`: the first block of every device has all 9 slots live.
All inputs are finite; a program needn't handle non-finite values.
Results may differ from a plain program's by a relative error of at most 0.0037.
Values sent between devices are 32-bit elements; how exact they have to be, the bound alone decides.
No kernel may reach another device: no remote copies, remote signals or barrier semaphores. Data moves between devices by JAX's collectives and lax.ppermute only.
A program may use at most 64 MiB of HBM per device.

v0:
```python
import jax
import jax.numpy as jnp
from jax import lax
from jax.sharding import PartitionSpec as P

BLK = 128
NP = 9
XP = 2
MYD = 128
MZ = 1024


def padded(cells, sides, width):
    for axis, dim in sides:
        count = lax.axis_size(axis)
        head = lax.slice_in_dim(cells, 0, width, axis=dim)
        tail = lax.slice_in_dim(cells, cells.shape[dim] - width, cells.shape[dim], axis=dim)
        cells = jnp.concatenate(
            [
                lax.ppermute(tail, axis, [(i, (i + 1) % count) for i in range(count)]),
                cells,
                lax.ppermute(head, axis, [((i + 1) % count, i) for i in range(count)]),
            ],
            axis=dim,
        )
    return cells


def shifted(x, axis, by):
    peers = lax.axis_size(axis)
    return lax.ppermute(x, axis, [(i, (i + by) % peers) for i in range(peers)])


def block_density(own_rows, partner_rows, slot_keep):
    distance_sq = sum(
        (
            (own_rows[component][:, :, None, None] - partner_rows[component][:, None, :, :]) ** 2
            for component in range(3)
        )
    )
    kernel = jnp.exp(-distance_sq / (own_rows[4] ** 2)[:, :, None, None])
    weights = partner_rows[3] * slot_keep[:, :, None]
    return jnp.sum(kernel * weights[:, None, :, :], axis=(2, 3)) * (1.0 / (NP * BLK))


def block_force(own_rows, partner_rows, slot_keep, own_term, partner_term):
    separations = [
        own_rows[component][:, :, None, None] - partner_rows[component][:, None, :, :]
        for component in range(3)
    ]
    distance_sq = separations[0] ** 2 + separations[1] ** 2 + separations[2] ** 2
    spread = 0.5 * ((own_rows[4] ** 2)[:, :, None, None] + (partner_rows[4] ** 2)[:, None, :, :])
    weights = partner_rows[3] * slot_keep[:, :, None]
    factor = (
        jnp.exp(-distance_sq / spread)
        / spread
        * (own_term[:, :, None, None] + partner_term[:, None, :, :])
        * weights[:, None, :, :]
        * (2.0 / (NP * BLK))
    )
    return jnp.stack([jnp.sum(factor * separation, axis=(2, 3)) for separation in separations])


def deposit(x_cells, y_cells, z_cells, offsets, masses, planes, group):
    total = x_cells.shape[0]
    rounds = total // group
    row_count = planes * (MYD + 1)
    row_ids = jnp.arange(row_count)
    depth_ids = jnp.arange(MZ)

    def accumulate(carry, inputs):
        cx_part, cy_part, cz_part, frac_part, mass_part = inputs
        table = jnp.zeros((group, row_count), jnp.float32)
        for shift_x in (0, 1):
            weight_x = frac_part[0] if shift_x else 1.0 - frac_part[0]
            for shift_y in (0, 1):
                weight_y = frac_part[1] if shift_y else 1.0 - frac_part[1]
                target = (cx_part + shift_x) * (MYD + 1) + cy_part + shift_y
                table = table + jnp.where(
                    row_ids[None, :] == target[:, None],
                    (mass_part * weight_x * weight_y)[:, None],
                    0.0,
                )
        loads = table.astype(jnp.bfloat16)
        lower_z = jnp.where(
            depth_ids[None, :] == cz_part[:, None], (1.0 - frac_part[2])[:, None], 0.0
        )
        upper_z = jnp.where(
            depth_ids[None, :] == ((cz_part + 1) % MZ)[:, None], frac_part[2][:, None], 0.0
        )
        depth = (lower_z + upper_z).astype(jnp.bfloat16)
        update = lax.dot_general(
            loads, depth, (((0,), (0,)), ((), ())), preferred_element_type=jnp.float32
        )
        return (carry + update, None)

    inputs = (
        x_cells.reshape(rounds, group),
        y_cells.reshape(rounds, group),
        z_cells.reshape(rounds, group),
        jnp.moveaxis(offsets.reshape(3, rounds, group), 1, 0),
        masses.reshape(rounds, group),
    )
    result, _ = lax.scan(accumulate, jnp.zeros((row_count, MZ), jnp.float32), inputs)
    return result


def on_device(positions, mass, smooth, cell_y, cell_z, cic_frac, pair_blocks, pair_count):
    count_blocks = pair_blocks.shape[0]
    half_blocks = count_blocks // 2
    rim_width = half_blocks * BLK
    per_plane = count_blocks // XP
    particle_count = count_blocks * BLK
    groups = count_blocks // 4
    state_rows = jnp.concatenate([positions, mass[None], smooth[None]], axis=0)
    extended = padded(state_rows, (("slab", 1),), rim_width)
    ext_blocks = extended.reshape(5, count_blocks + 2 * half_blocks, BLK)
    own_groups = jnp.moveaxis(state_rows.reshape(5, groups, 4, BLK), 1, 0)
    slot_mask = (jnp.arange(NP)[None, :] < pair_count[:, None]).astype(jnp.float32)
    index_groups = pair_blocks.reshape(groups, 4, NP)
    mask_groups = slot_mask.reshape(groups, 4, NP)

    def density_step(inputs):
        own_rows, partner_ids, slot_keep = inputs
        return block_density(own_rows, ext_blocks[:, partner_ids], slot_keep)

    density = lax.map(density_step, (own_groups, index_groups, mask_groups)).reshape(particle_count)
    pressure_term = density ** (-1.0 / 3.0)
    term_ext = padded(pressure_term, (("slab", 0),), rim_width).reshape(-1, BLK)
    term_groups = pressure_term.reshape(groups, 4, BLK)

    def force_step(inputs):
        own_rows, partner_ids, slot_keep, own_term = inputs
        return block_force(
            own_rows, ext_blocks[:, partner_ids], slot_keep, own_term, term_ext[partner_ids]
        )

    acceleration = lax.map(force_step, (own_groups, index_groups, mask_groups, term_groups))
    acceleration = jnp.moveaxis(acceleration, 1, 0).reshape(3, particle_count)
    x_cells = jnp.arange(particle_count) // BLK // per_plane
    layer = deposit(x_cells, cell_y, cell_z, cic_frac, mass, XP + 1, 512).reshape(
        XP + 1, MYD + 1, MZ
    )
    incoming = shifted(layer[XP], "slab", 1)
    grid = layer[:XP].at[0].add(incoming)
    rim_rows = shifted(grid[:, MYD], "col", 1)
    grid = grid[:, :MYD].at[:, 0].add(rim_rows)
    return (density, acceleration, grid)


def solution(mesh):
    return jax.shard_map(
        on_device,
        mesh=mesh,
        in_specs=(
            P(None, ("slab", "col")),
            P(("slab", "col")),
            P(("slab", "col")),
            P(("slab", "col")),
            P(("slab", "col")),
            P(None, ("slab", "col")),
            P(("slab", "col"), None),
            P(("slab", "col")),
        ),
        out_specs=(P(("slab", "col")), P(None, ("slab", "col")), P("slab", "col", None)),
        check_vma=False,
    )
```

profile of v0, /device:TPU:8, one launch (start us, length us, event | category | flops | bytes accessed | tf_op | source)
XLA Modules:
  0.0 264.3 jit_solution(10551511931095750249)
XLA Ops:
  4.3 13.3 %collective-permute-start.1 = (f32[5,4096]{1,0:T(8,128)}, f32[5,4096]{1,0:T(8,128)}, u32[]{:S(2)}, u32[]{:S(2)}) collective-permute-start(f32[5,4096]{1,0:T(8,128)} %get-tuple-element.385), channel_id=1, source_target_pairs={{8,0},{16,8},{24,16},{32,24},{40,32},{48,40},{56,48},{64,56},{72,6... | collective-permute-start | bytes 245768 | tf_op jit(solution)/shard_map/ppermute | solution.py:22
  20.0 47.2 %while.38 = (s32[]{:T(128)}, f32[387,1024]{1,0:T(8,128)S(1)}, s32[16,512]{1,0:T(8,128)S(1)}, s32[16,512]{1,0:T(8,128)S(1)}, f32[16,512]{1,0:T(8,128)S(1)}, /*ind...) while((s32[]{:T(128)}, f32[387,1024]{1,0:T(8,128)S(1)}, ...), condition=%wide.region_9.10_spmd.clone.clone, body=%wide.region_8.9_spmd.clone.clone.sunk | while | flops 412129280 | bytes 3254443 | solution.py:104
  23.8 2.0 select_add_fusion.2
  26.8 2.0 select_add_fusion.2
  29.7 2.0 select_add_fusion.2
  35.6 2.0 select_add_fusion.2
  41.5 2.0 select_add_fusion.2
  44.5 2.0 select_add_fusion.2
  47.4 2.0 select_add_fusion.2
  50.4 2.0 select_add_fusion.2
  56.2 2.0 select_add_fusion.2
  65.1 2.0 select_add_fusion.2
  74.3 68.5 %while.36 = (s32[]{:T(128)}, f32[16,4,128]{2,1,0:T(4,128)S(1)}, f32[16,5,4,128]{3,2,1,0:T(4,128)}, s32[16,4,9]{2,1,0:T(4,128)}, f32[5,128,128]{2,0,1:T(8,128)S(1...) while((s32[]{:T(128)}, f32[16,4,128]{2,1,0:T(4,128)S(1)}, ...), condition=%wide.region_2.3_spmd, body=%wide.region_0.2_spmd.sunk | while | flops 7084145 | bytes 626117 | solution.py:127
  144.8 7.3 %collective-permute-start.3 = (f32[4096]{0:T(1024)S(1)}, f32[4096]{0:T(1024)S(1)}, u32[]{:S(2)}, u32[]{:S(2)}) collective-permute-start(f32[4096]{0:T(1024)S(1)} %get-tuple-element.387), channel_id=1, source_target_pairs={{8,0},{16,8},{24,16},{32,24},{40,32},{48,40},{56,48},{64,56},{72,6... | collective-permute-start | bytes 49160 | tf_op jit(solution)/shard_map/ppermute | solution.py:22
  154.7 3.5 %collective-permute-start.5 = (f32[2,1024]{1,0:T(2,128)S(1)}, f32[2,1024]{1,0:T(2,128)S(1)}, u32[]{:S(2)}, u32[]{:S(2)}) collective-permute-start(f32[2,1024]{1,0:T(2,128)S(1)} %bitcast.183), channel_id=1, source_target_pairs={{0,1},{1,2},{2,3},{3,4},{4,5},{5,6},{6,7},{7,0},{8,9},{9,10},{10,1... | collective-permute-start | bytes 24584 | tf_op jit(solution)/shard_map/ppermute | solution.py:31
  158.2 104.2 %while.37 = (s32[]{:T(128)}, f32[16,3,4,128]{3,2,1,0:T(4,128)S(1)}, f32[16,5,4,128]{3,2,1,0:T(4,128)}, s32[16,4,9]{2,1,0:T(4,128)}, f32[5,128,128]{2,0,1:T(8,128...) while((s32[]{:T(128)}, f32[16,3,4,128]{3,2,1,0:T(4,128)S(1)}, ...), condition=%wide.region_7.8_spmd, body=%wide.region_3.7_spmd.sunk | while | flops 13578353 | bytes 792169 | solution.py:138
  161.6 3.0 %fusion.51 = (f32[4,128]{1,0:T(4,128)S(1)}, f32[4,128]{1,0:T(4,128)S(1)}, f32[4,128]{1,0:T(4,128)S(1)}) fusion(f32[4,9,128]{2,1,0:T(8,128)S(1)} %get-tuple-element.546, f32[4,128]{1,0:T(4,128)S(1)} %get-tuple-element.547, f32[4,9,128]{2,1,0:T(8,128)S(1)} %fusion.50, f32[4,9,128]{2,1,0:T(8,128)S(1)} %reshape.495, ...), kind=kLoop, calls=%fused_computation.33.clone.1 | loop fusion | flops 13564416 | bytes 126976 | tf_op jit(solution)/shard_map/while/body/eval_jaxpr/reduce_sum | solution.py:61
  168.1 3.0 %fusion.51 = (f32[4,128]{1,0:T(4,128)S(1)}, f32[4,128]{1,0:T(4,128)S(1)}, f32[4,128]{1,0:T(4,128)S(1)}) fusion(f32[4,9,128]{2,1,0:T(8,128)S(1)} %get-tuple-element.546, f32[4,128]{1,0:T(4,128)S(1)} %get-tuple-element.547, f32[4,9,128]{2,1,0:T(8,128)S(1)} %fusion.50, f32[4,9,128]{2,1,0:T(8,128)S(1)} %reshape.495, ...), kind=kLoop, calls=%fused_computation.33.clone.1 | loop fusion | flops 13564416 | bytes 126976 | tf_op jit(solution)/shard_map/while/body/eval_jaxpr/reduce_sum | solution.py:61
  174.6 3.0 %fusion.51 = (f32[4,128]{1,0:T(4,128)S(1)}, f32[4,128]{1,0:T(4,128)S(1)}, f32[4,128]{1,0:T(4,128)S(1)}) fusion(f32[4,9,128]{2,1,0:T(8,128)S(1)} %get-tuple-element.546, f32[4,128]{1,0:T(4,128)S(1)} %get-tuple-element.547, f32[4,9,128]{2,1,0:T(8,128)S(1)} %fusion.50, f32[4,9,128]{2,1,0:T(8,128)S(1)} %reshape.495, ...), kind=kLoop, calls=%fused_computation.33.clone.1 | loop fusion | flops 13564416 | bytes 126976 | tf_op jit(solution)/shard_map/while/body/eval_jaxpr/reduce_sum | solution.py:61
  181.1 3.0 %fusion.51 = (f32[4,128]{1,0:T(4,128)S(1)}, f32[4,128]{1,0:T(4,128)S(1)}, f32[4,128]{1,0:T(4,128)S(1)}) fusion(f32[4,9,128]{2,1,0:T(8,128)S(1)} %get-tuple-element.546, f32[4,128]{1,0:T(4,128)S(1)} %get-tuple-element.547, f32[4,9,128]{2,1,0:T(8,128)S(1)} %fusion.50, f32[4,9,128]{2,1,0:T(8,128)S(1)} %reshape.495, ...), kind=kLoop, calls=%fused_computation.33.clone.1 | loop fusion | flops 13564416 | bytes 126976 | tf_op jit(solution)/shard_map/while/body/eval_jaxpr/reduce_sum | solution.py:61
  187.6 3.0 %fusion.51 = (f32[4,128]{1,0:T(4,128)S(1)}, f32[4,128]{1,0:T(4,128)S(1)}, f32[4,128]{1,0:T(4,128)S(1)}) fusion(f32[4,9,128]{2,1,0:T(8,128)S(1)} %get-tuple-element.546, f32[4,128]{1,0:T(4,128)S(1)} %get-tuple-element.547, f32[4,9,128]{2,1,0:T(8,128)S(1)} %fusion.50, f32[4,9,128]{2,1,0:T(8,128)S(1)} %reshape.495, ...), kind=kLoop, calls=%fused_computation.33.clone.1 | loop fusion | flops 13564416 | bytes 126976 | tf_op jit(solution)/shard_map/while/body/eval_jaxpr/reduce_sum | solution.py:61
  194.2 3.0 %fusion.51 = (f32[4,128]{1,0:T(4,128)S(1)}, f32[4,128]{1,0:T(4,128)S(1)}, f32[4,128]{1,0:T(4,128)S(1)}) fusion(f32[4,9,128]{2,1,0:T(8,128)S(1)} %get-tuple-element.546, f32[4,128]{1,0:T(4,128)S(1)} %get-tuple-element.547, f32[4,9,128]{2,1,0:T(8,128)S(1)} %fusion.50, f32[4,9,128]{2,1,0:T(8,128)S(1)} %reshape.495, ...), kind=kLoop, calls=%fused_computation.33.clone.1 | loop fusion | flops 13564416 | bytes 126976 | tf_op jit(solution)/shard_map/while/body/eval_jaxpr/reduce_sum | solution.py:61
  200.7 3.0 %fusion.51 = (f32[4,128]{1,0:T(4,128)S(1)}, f32[4,128]{1,0:T(4,128)S(1)}, f32[4,128]{1,0:T(4,128)S(1)}) fusion(f32[4,9,128]{2,1,0:T(8,128)S(1)} %get-tuple-element.546, f32[4,128]{1,0:T(4,128)S(1)} %get-tuple-element.547, f32[4,9,128]{2,1,0:T(8,128)S(1)} %fusion.50, f32[4,9,128]{2,1,0:T(8,128)S(1)} %reshape.495, ...), kind=kLoop, calls=%fused_computation.33.clone.1 | loop fusion | flops 13564416 | bytes 126976 | tf_op jit(solution)/shard_map/while/body/eval_jaxpr/reduce_sum | solution.py:61
  207.2 3.0 %fusion.51 = (f32[4,128]{1,0:T(4,128)S(1)}, f32[4,128]{1,0:T(4,128)S(1)}, f32[4,128]{1,0:T(4,128)S(1)}) fusion(f32[4,9,128]{2,1,0:T(8,128)S(1)} %get-tuple-element.546, f32[4,128]{1,0:T(4,128)S(1)} %get-tuple-element.547, f32[4,9,128]{2,1,0:T(8,128)S(1)} %fusion.50, f32[4,9,128]{2,1,0:T(8,128)S(1)} %reshape.495, ...), kind=kLoop, calls=%fused_computation.33.clone.1 | loop fusion | flops 13564416 | bytes 126976 | tf_op jit(solution)/shard_map/while/body/eval_jaxpr/reduce_sum | solution.py:61
  213.7 3.0 %fusion.51 = (f32[4,128]{1,0:T(4,128)S(1)}, f32[4,128]{1,0:T(4,128)S(1)}, f32[4,128]{1,0:T(4,128)S(1)}) fusion(f32[4,9,128]{2,1,0:T(8,128)S(1)} %get-tuple-element.546, f32[4,128]{1,0:T(4,128)S(1)} %get-tuple-element.547, f32[4,9,128]{2,1,0:T(8,128)S(1)} %fusion.50, f32[4,9,128]{2,1,0:T(8,128)S(1)} %reshape.495, ...), kind=kLoop, calls=%fused_computation.33.clone.1 | loop fusion | flops 13564416 | bytes 126976 | tf_op jit(solution)/shard_map/while/body/eval_jaxpr/reduce_sum | solution.py:61
  220.2 3.0 %fusion.51 = (f32[4,128]{1,0:T(4,128)S(1)}, f32[4,128]{1,0:T(4,128)S(1)}, f32[4,128]{1,0:T(4,128)S(1)}) fusion(f32[4,9,128]{2,1,0:T(8,128)S(1)} %get-tuple-element.546, f32[4,128]{1,0:T(4,128)S(1)} %get-tuple-element.547, f32[4,9,128]{2,1,0:T(8,128)S(1)} %fusion.50, f32[4,9,128]{2,1,0:T(8,128)S(1)} %reshape.495, ...), kind=kLoop, calls=%fused_computation.33.clone.1 | loop fusion | flops 13564416 | bytes 126976 | tf_op jit(solution)/shard_map/while/body/eval_jaxpr/reduce_sum | solution.py:61
  226.8 3.0 %fusion.51 = (f32[4,128]{1,0:T(4,128)S(1)}, f32[4,128]{1,0:T(4,128)S(1)}, f32[4,128]{1,0:T(4,128)S(1)}) fusion(f32[4,9,128]{2,1,0:T(8,128)S(1)} %get-tuple-element.546, f32[4,128]{1,0:T(4,128)S(1)} %get-tuple-element.547, f32[4,9,128]{2,1,0:T(8,128)S(1)} %fusion.50, f32[4,9,128]{2,1,0:T(8,128)S(1)} %reshape.495, ...), kind=kLoop, calls=%fused_computation.33.clone.1 | loop fusion | flops 13564416 | bytes 126976 | tf_op jit(solution)/shard_map/while/body/eval_jaxpr/reduce_sum | solution.py:61
  233.3 3.0 %fusion.51 = (f32[4,128]{1,0:T(4,128)S(1)}, f32[4,128]{1,0:T(4,128)S(1)}, f32[4,128]{1,0:T(4,128)S(1)}) fusion(f32[4,9,128]{2,1,0:T(8,128)S(1)} %get-tuple-element.546, f32[4,128]{1,0:T(4,128)S(1)} %get-tuple-element.547, f32[4,9,128]{2,1,0:T(8,128)S(1)} %fusion.50, f32[4,9,128]{2,1,0:T(8,128)S(1)} %reshape.495, ...), kind=kLoop, calls=%fused_computation.33.clone.1 | loop fusion | flops 13564416 | bytes 126976 | tf_op jit(solution)/shard_map/while/body/eval_jaxpr/reduce_sum | solution.py:61
  239.7 3.0 %fusion.51 = (f32[4,128]{1,0:T(4,128)S(1)}, f32[4,128]{1,0:T(4,128)S(1)}, f32[4,128]{1,0:T(4,128)S(1)}) fusion(f32[4,9,128]{2,1,0:T(8,128)S(1)} %get-tuple-element.546, f32[4,128]{1,0:T(4,128)S(1)} %get-tuple-element.547, f32[4,9,128]{2,1,0:T(8,128)S(1)} %fusion.50, f32[4,9,128]{2,1,0:T(8,128)S(1)} %reshape.495, ...), kind=kLoop, calls=%fused_computation.33.clone.1 | loop fusion | flops 13564416 | bytes 126976 | tf_op jit(solution)/shard_map/while/body/eval_jaxpr/reduce_sum | solution.py:61
  246.3 3.0 %fusion.51 = (f32[4,128]{1,0:T(4,128)S(1)}, f32[4,128]{1,0:T(4,128)S(1)}, f32[4,128]{1,0:T(4,128)S(1)}) fusion(f32[4,9,128]{2,1,0:T(8,128)S(1)} %get-tuple-element.546, f32[4,128]{1,0:T(4,128)S(1)} %get-tuple-element.547, f32[4,9,128]{2,1,0:T(8,128)S(1)} %fusion.50, f32[4,9,128]{2,1,0:T(8,128)S(1)} %reshape.495, ...), kind=kLoop, calls=%fused_computation.33.clone.1 | loop fusion | flops 13564416 | bytes 126976 | tf_op jit(solution)/shard_map/while/body/eval_jaxpr/reduce_sum | solution.py:61
  252.8 3.0 %fusion.51 = (f32[4,128]{1,0:T(4,128)S(1)}, f32[4,128]{1,0:T(4,128)S(1)}, f32[4,128]{1,0:T(4,128)S(1)}) fusion(f32[4,9,128]{2,1,0:T(8,128)S(1)} %get-tuple-element.546, f32[4,128]{1,0:T(4,128)S(1)} %get-tuple-element.547, f32[4,9,128]{2,1,0:T(8,128)S(1)} %fusion.50, f32[4,9,128]{2,1,0:T(8,128)S(1)} %reshape.495, ...), kind=kLoop, calls=%fused_computation.33.clone.1 | loop fusion | flops 13564416 | bytes 126976 | tf_op jit(solution)/shard_map/while/body/eval_jaxpr/reduce_sum | solution.py:61
  259.3 3.0 %fusion.51 = (f32[4,128]{1,0:T(4,128)S(1)}, f32[4,128]{1,0:T(4,128)S(1)}, f32[4,128]{1,0:T(4,128)S(1)}) fusion(f32[4,9,128]{2,1,0:T(8,128)S(1)} %get-tuple-element.546, f32[4,128]{1,0:T(4,128)S(1)} %get-tuple-element.547, f32[4,9,128]{2,1,0:T(8,128)S(1)} %fusion.50, f32[4,9,128]{2,1,0:T(8,128)S(1)} %reshape.495, ...), kind=kLoop, calls=%fused_computation.33.clone.1 | loop fusion | flops 13564416 | bytes 126976 | tf_op jit(solution)/shard_map/while/body/eval_jaxpr/reduce_sum | solution.py:61
  (562 shorter events, 168.4 us)
Async XLA Ops:
  2.4 70.8 %collective-permute-start = (f32[5,4096]{1,0:T(8,128)}, f32[5,4096]{1,0:T(8,128)}, u32[]{:S(2)}, u32[]{:S(2)}) collective-permute-start(f32[5,4096]{1,0:T(8,128)} %get-tuple-element.384), channel_id=1, source_target_pairs={{0,8},{8,16},{16,24},{24,32},{32,40},{40,48},{48,56},{56,64},{64,7... | collective-permute-start | bytes 245768 | tf_op jit(solution)/shard_map/ppermute | solution.py:20
  4.3 68.9 %collective-permute-start.1 = (f32[5,4096]{1,0:T(8,128)}, f32[5,4096]{1,0:T(8,128)}, u32[]{:S(2)}, u32[]{:S(2)}) collective-permute-start(f32[5,4096]{1,0:T(8,128)} %get-tuple-element.385), channel_id=1, source_target_pairs={{8,0},{16,8},{24,16},{32,24},{40,32},{48,40},{56,48},{64,56},{72,6... | collective-permute-start | bytes 245768 | tf_op jit(solution)/shard_map/ppermute | solution.py:22
  20.0 50.0 %copy-start.1 = (f32[3,8192]{1,0:T(4,128)S(1)}, f32[3,8192]{1,0:T(4,128)}, u32[]{:S(2)}) copy-start(f32[3,8192]{1,0:T(4,128)} %param.18) | copy-start | bytes 294916
  67.2 3.0 %copy-start = (f32[387,1024]{1,0:T(8,128)}, f32[387,1024]{1,0:T(8,128)S(1)}, u32[]{:S(2)}) copy-start(f32[387,1024]{1,0:T(8,128)S(1)} %get-tuple-element.229) | copy-start | bytes 4755460
  67.2 4.5 %copy-start.9 = (s32[64,9]{0,1:T(8,128)S(1)}, s32[64,9]{0,1:T(8,128)}, u32[]{:S(2)}) copy-start(s32[64,9]{0,1:T(8,128)} %param.24) | copy-start | bytes 6916
  67.2 5.1 %copy-start.3 = (f32[8192]{0:T(1024)S(1)}, f32[8192]{0:T(1024)}, u32[]{:S(2)}) copy-start(f32[8192]{0:T(1024)} %param.19) | copy-start | bytes 98308
  67.2 5.1 %copy-start.4 = (f32[8192]{0:T(1024)S(1)}, f32[8192]{0:T(1024)}, u32[]{:S(2)}) copy-start(f32[8192]{0:T(1024)} %param.20) | copy-start | bytes 98308
  68.1 85.4 %collective-permute-start.4 = (f32[129,1024]{1,0:T(8,128)}, f32[129,1024]{1,0:T(8,128)S(1)}, u32[]{:S(2)}, u32[]{:S(2)}) collective-permute-start(f32[129,1024]{1,0:T(8,128)} %slice.167), channel_id=1, source_target_pairs={{0,8},{8,16},{16,24},{24,32},{32,40},{40,48},{48,56},{56,64},{64,7... | collective-permute-start | bytes 1585160 | tf_op jit(solution)/shard_map/ppermute | solution.py:31
  72.4 0.8 copy-start.5
  73.1 1.2 copy-start.6
  142.8 15.4 %copy-start.7 = (f32[16,4,128]{2,1,0:T(4,128)}, f32[16,4,128]{2,1,0:T(4,128)S(1)}, u32[]{:S(2)}) copy-start(f32[16,4,128]{2,1,0:T(4,128)S(1)} %get-tuple-element.227) | copy-start | bytes 98308
  142.8 15.3 %copy-start.8 = (f32[16,3,4,128]{3,2,1,0:T(4,128)S(1)}, f32[16,3,4,128]{3,2,1,0:T(4,128)}, u32[]{:S(2)}) copy-start(f32[16,3,4,128]{3,2,1,0:T(4,128)} %custom-call.8) | copy-start | bytes 294916
  142.9 9.3 %collective-permute-start.2 = (f32[4096]{0:T(1024)S(1)}, f32[4096]{0:T(1024)S(1)}, u32[]{:S(2)}, u32[]{:S(2)}) collective-permute-start(f32[4096]{0:T(1024)S(1)} %get-tuple-element.386), channel_id=1, source_target_pairs={{0,8},{8,16},{16,24},{24,32},{32,40},{40,48},{48,56},{56,64},{64,7... | collective-permute-start | bytes 49160 | tf_op jit(solution)/shard_map/ppermute | solution.py:20
  144.8 8.7 %collective-permute-start.3 = (f32[4096]{0:T(1024)S(1)}, f32[4096]{0:T(1024)S(1)}, u32[]{:S(2)}, u32[]{:S(2)}) collective-permute-start(f32[4096]{0:T(1024)S(1)} %get-tuple-element.387), channel_id=1, source_target_pairs={{8,0},{16,8},{24,16},{32,24},{40,32},{48,40},{56,48},{64,56},{72,6... | collective-permute-start | bytes 49160 | tf_op jit(solution)/shard_map/ppermute | solution.py:22
  154.7 108.5 %collective-permute-start.5 = (f32[2,1024]{1,0:T(2,128)S(1)}, f32[2,1024]{1,0:T(2,128)S(1)}, u32[]{:S(2)}, u32[]{:S(2)}) collective-permute-start(f32[2,1024]{1,0:T(2,128)S(1)} %bitcast.183), channel_id=1, source_target_pairs={{0,1},{1,2},{2,3},{3,4},{4,5},{5,6},{6,7},{7,0},{8,9},{9,10},{10,1... | collective-permute-start | bytes 24584 | tf_op jit(solution)/shard_map/ppermute | solution.py:31
  263.3 1.0 copy-start.2
where the time goes:
time: 268 us; the launch traced here: 264 us
  other arithmetic  123 us (46%)
  local copies, waits for them, and re-layouts  75.1 us (28%)
  matrix products  32.1 us (12%)
  starting transfers between devices  29.8 us (11%)
    reduce_sum x16, other arithmetic, block_force(): jnp.sum(factor * separation, axis=(2, 3))  48.4 us
    dot_general x16, matrix products, accumulate(): lax.dot_general(loads, depth, (((0,), (0,)), ((), ())), preferred_element...  32.1 us
    reduce_sum x16, other arithmetic, block_density(): jnp.sum(kernel * weights[:, None, :, :], axis=(2, 3)) * (1.0 / (NP * BLK))  22.3 us
    ppermute x2, starting transfers between devices, padded(): lax.ppermute(head, axis, [((i + 1) % count, i) for i in range(count)])  20.6 us
    slice x16, local copies, waits for them, and re-layouts, accumulate(): weight_x = frac_part[0] if shift_x else 1.0 - frac_part[0]  13.2 us
    sub x32, other arithmetic, block_force(): own_rows[component][:, :, None, None]  11.3 us
    sub x16, other arithmetic, block_density(): own_rows[component][:, :, None, None]  11.1 us
    select_n x16, other arithmetic, density_step(): return block_density(own_rows, ext_blocks[:, partner_ids], slot_keep)  10.8 us
  transfers between devices with their start and end apart: 6, of which 1 were waited for; matrix products, arithmetic and copies ran while one was open for 85% of the time, Pallas kernels for 0%

commit v1 on v0

v1 whole, which is shorter than its diff:
```python
import functools
import jax
import jax.numpy as jnp
from jax import lax
from jax.sharding import PartitionSpec as P
from jax.experimental import pallas as pl
from jax.experimental.pallas import tpu as pltpu

BLK=128; NP=9; XP=2; MYD=128; MZ=1024
LOG2E=1.4426950408889634
f32=jnp.float32; bf16=jnp.bfloat16

def split3(x):
    h=x.astype(bf16).astype(f32)
    r=x-h
    m=r.astype(bf16).astype(f32)
    l=(r-m)
    return h,m,l

def feats(st):
    x=st[0:3]; m=st[3:4]; s=st[4:5]
    n=x[0:1]*x[0:1]+x[1:2]*x[1:2]+x[2:3]*x[2:3]
    one=jnp.ones_like(m)
    return x,n,m,s,one

def stack_a(h,m,l):
    z=jnp.zeros((80,h.shape[1]),f32)
    return jnp.concatenate([h,h,m,m,h,l,z],0)
def stack_b(h,m,l):
    z=jnp.zeros((80,h.shape[1]),f32)
    return jnp.concatenate([h,m,h,m,l,h,z],0)

def build_list(pb,pc,lst,G,count):
    def body(b,pos):
        for k in range(NP):
            lst[pos+k]=pb[b,k]+b*256
        return pos+pc[b]
    n=lax.fori_loop(0,count,body,jnp.int32(0))
    for k in range(G):
        lst[n+k]=jnp.int32(count*256)
    return (n+G-1)//G

def prep_a(src,a_ref,at,nb):
    def body(i,_):
        st=src[:,pl.ds(pl.multiple_of(i*128,128),128)]
        x,n,m,s,one=feats(st)
        s8=jnp.concatenate([x,n,jnp.log2(m),0.5*s*s,one,jnp.zeros_like(one)],0)
        a=stack_a(*split3(s8))
        a_ref[at+i]=a.T.astype(bf16)
        return 0
    lax.fori_loop(0,nb,body,0,unroll=4)

def density_kernel(G,own,lo,hi,pb,pc,den,term,a_ref,b_ref,acc,lst):
    nb=den.shape[0]; hb=nb//2
    nit=build_list(pb,pc,lst,G,nb)
    prep_a(lo,a_ref,0,hb); prep_a(own,a_ref,hb,nb); prep_a(hi,a_ref,hb+nb,hb)
    def bb(i,_):
        st=own[:,pl.ds(pl.multiple_of(i*128,128),128)]
        x,n,m,s,one=feats(st)
        c=LOG2E/(s*s)
        b8=jnp.concatenate([2*c*x,-c,one,jnp.zeros_like(one),-c*n,jnp.zeros_like(one)],0)
        b_ref[i]=stack_b(*split3(b8)).astype(bf16)
        return 0
    lax.fori_loop(0,nb,bb,0,unroll=4)
    b_ref[nb]=jnp.zeros((128,128),bf16)
    acc[...]=jnp.zeros_like(acc)
    def main(it,_):
        for g in range(G):
            code=lst[it*G+g]
            b=code>>8; p=code&255
            e=jnp.dot(a_ref[p],b_ref[b],preferred_element_type=f32)
            q=jnp.exp2(e)
            acc[b]+=q.reshape(16,8,128).sum(0)
        return 0
    lax.fori_loop(0,nit,main,0)
    d=acc[0:nb].sum(1)*(1.0/(NP*BLK))
    den[...]=d
    term[...]=jnp.exp2(jnp.log2(d)*(-1.0/3.0))

def density(own,lo,hi,pb,pc,G=8):
    nb=pb.shape[0]
    V=pl.BlockSpec(memory_space=pltpu.VMEM); S=pl.BlockSpec(memory_space=pltpu.SMEM)
    return pl.pallas_call(functools.partial(density_kernel,G),
        out_shape=[jax.ShapeDtypeStruct((nb,128),f32)]*2,
        in_specs=[V,V,V,S,S],out_specs=[V,V],
        scratch_shapes=[pltpu.VMEM((2*nb,128,128),bf16),pltpu.VMEM((nb+1,128,128),bf16),pltpu.VMEM((nb+1,8,128),f32),
                        pltpu.SMEM((nb*NP+NP+2*G,),jnp.int32)],
        compiler_params=pltpu.CompilerParams(vmem_limit_bytes=48<<20),
        name="density")(own,lo,hi,pb,pc)

def force_kernel(G,own,lo,hi,town,tlo,thi,pb,pc,out,a_ref,b_ref,v_ref,acc,lst):
    nb=town.shape[0]; hb=nb//2
    nit=build_list(pb,pc,lst,G,nb)
    prep_a(lo,a_ref,0,hb); prep_a(own,a_ref,hb,nb); prep_a(hi,a_ref,hb+nb,hb)
    def pv(src,t,at,n_):
        def body(i,_):
            st=src[:,pl.ds(pl.multiple_of(i*128,128),128)]
            x=st[0:3]; m=st[3:4]
            mt=m*t[pl.ds(i,1),:]
            v=jnp.concatenate([m,m*x,mt,mt*x],0)
            h=v.astype(bf16)
            l=(v-h.astype(f32)).astype(bf16)
            v_ref[at+i]=jnp.concatenate([h.astype(f32),l.astype(f32)],0).astype(bf16)
            return 0
        lax.fori_loop(0,n_,body,0,unroll=4)
    pv(lo,tlo,0,hb); pv(own,town,hb,nb); pv(hi,thi,hb+nb,hb)
    def bb(i,_):
        st=own[:,pl.ds(pl.multiple_of(i*128,128),128)]
        x,n,m,s,one=feats(st)
        z=jnp.zeros_like(one)
        b8=jnp.concatenate([(2*LOG2E)*x,-LOG2E*one,z,z,-LOG2E*n,z],0)
        c8=jnp.concatenate([z,z,z,z,z,one,0.5*s*s,z],0)
        b_ref[i,:,0:128]=stack_b(*split3(b8)).astype(bf16)
        b_ref[i,:,128:256]=stack_b(*split3(c8)).astype(bf16)
        return 0
    lax.fori_loop(0,nb,bb,0,unroll=4)
    b_ref[nb]=jnp.ones((128,256),bf16)
    acc[...]=jnp.zeros_like(acc)
    def main(it,_):
        L=4
        cs=[lst[it*G+g] for g in range(G)]
        qs={}; es={}
        def d1(g):
            es[g]=jnp.dot(a_ref[cs[g]&255],b_ref[cs[g]>>8],preferred_element_type=f32)
        def qq(g):
            e=es.pop(g)
            rs=pl.reciprocal(e[:,128:256],approx=True)
            qs[g]=(jnp.exp2(e[:,0:128]*rs)*rs).astype(bf16)
        def d2(g):
            acc[cs[g]>>8]+=jnp.dot(v_ref[cs[g]&255],qs.pop(g),preferred_element_type=f32)
        for s in range(G+2*L):
            if s<G: d1(s)
            if 0<=s-L<G: qq(s-L)
            if 0<=s-2*L<G: d2(s-2*L)
        return 0
    lax.fori_loop(0,nit,main,0)
    def fin(i,_):
        a=acc[i]
        s8=a[0:8]+a[8:16]
        x=own[0:3,pl.ds(pl.multiple_of(i*128,128),128)]
        t=town[pl.ds(i,1),:]
        f=t*(x*s8[0:1]-s8[1:4])+(x*s8[4:5]-s8[5:8])
        out[:,pl.ds(pl.multiple_of(i*128,128),128)]=f*(2.0/(NP*BLK))
        return 0
    lax.fori_loop(0,nb,fin,0,unroll=4)

def force(own,lo,hi,town,tlo,thi,pb,pc,G=8):
    nb=pb.shape[0]
    V=pl.BlockSpec(memory_space=pltpu.VMEM); S=pl.BlockSpec(memory_space=pltpu.SMEM)
    return pl.pallas_call(functools.partial(force_kernel,G),
        out_shape=jax.ShapeDtypeStruct((3,nb*128),f32),
        in_specs=[V]*6+[S,S],out_specs=V,
        scratch_shapes=[pltpu.VMEM((2*nb,128,128),bf16),pltpu.VMEM((nb+1,128,256),bf16),pltpu.VMEM((2*nb,16,128),bf16),
                        pltpu.VMEM((nb+1,16,128),f32),
                        pltpu.SMEM((nb*NP+NP+2*G,),jnp.int32)],
        compiler_params=pltpu.CompilerParams(vmem_limit_bytes=48<<20),
        name="force")(own,lo,hi,town,tlo,thi,pb,pc)
i16=jnp.int16

def depth_table(iz,cz,fz,kc):
    a=cz.astype(i16); b=((cz+1)&(MZ-1)).astype(i16)
    w0=(1.0-fz).astype(bf16); w1=fz.astype(bf16)
    return jnp.where(iz==a,w0,jnp.where(iz==b,w1,jnp.zeros_like(w1)))

def plane_rows(iy,cy,w_lo,w_hi):
    a=cy.astype(i16); b=(cy+1).astype(i16)
    z=jnp.zeros_like(w_lo)
    return jnp.where(iy==a,w_lo,jnp.where(iy==b,w_hi,z))

def deposit_own_kernel(kc,st,grid,rim):
    n=st.shape[1]; half=n//2
    iz=lax.broadcasted_iota(i16,(MZ,kc),0)
    iy=lax.broadcasted_iota(i16,(128,kc),0)
    def parts(at):
        s=st[:,pl.ds(at,kc)]
        m=s[3:4]; cy=s[5:6].astype(jnp.int32); cz=s[6:7].astype(jnp.int32)
        return m,cy,cz,s[7:8],s[8:9],s[9:10]
    def rowset(m,wx,cy,fy):
        mx=m*wx
        lo=(mx*(1.0-fy)).astype(bf16); hi=(mx*fy).astype(bf16)
        main=plane_rows(iy,cy,lo,hi)
        edge=jnp.where(cy.astype(i16)==127,hi,jnp.zeros_like(hi))
        return main,edge
    grid[...]=jnp.zeros_like(grid); rim[...]=jnp.zeros_like(rim)
    nt=(((1,),(1,)),((),()))
    it=lax.broadcasted_iota(i16,(16,kc),0)
    def first(i,_):
        m,cy,cz,fx,fy,fz=parts(pl.multiple_of(i*kc,128))
        d=depth_table(iz,cz,fz,kc)
        a0,e0=rowset(m,1.0-fx,cy,fy)
        a1,e1=rowset(m,fx,cy,fy)
        zz=jnp.zeros_like(it).astype(bf16)
        ed=jnp.where(it==0,e0,jnp.where(it==1,e1,zz))
        l=jnp.concatenate([a0,a1,ed],0)
        u=lax.dot_general(l,d,nt,preferred_element_type=f32)
        grid[0]+=u[0:128]; grid[1]+=u[128:256]; rim[...]+=u[256:264]
        return 0
    lax.fori_loop(0,half//kc,first,0)
    def second(i,_):
        m,cy,cz,fx,fy,fz=parts(pl.multiple_of(half+i*kc,128))
        d=depth_table(iz,cz,fz,kc)
        a1,e1=rowset(m,1.0-fx,cy,fy)
        zz=jnp.zeros_like(it).astype(bf16)
        l=jnp.concatenate([a1,jnp.where(it==1,e1,zz)],0)
        u=lax.dot_general(l,d,nt,preferred_element_type=f32)
        grid[1]+=u[0:128]; rim[...]+=u[128:136]
        return 0
    lax.fori_loop(0,half//kc,second,0)

def deposit_in_kernel(kc,st,g_in,r_in,grid,rim):
    n=st.shape[1]
    iz=lax.broadcasted_iota(i16,(MZ,kc),0)
    iy=lax.broadcasted_iota(i16,(128,kc),0)
    nt=(((1,),(1,)),((),()))
    it=lax.broadcasted_iota(i16,(16,kc),0)
    grid[...]=g_in[...]; rim[...]=r_in[...]
    def body(i,_):
        s=st[:,pl.ds(pl.multiple_of(i*kc,128),kc)]
        m=s[3:4]; cy=s[5:6].astype(jnp.int32); cz=s[6:7].astype(jnp.int32)
        mx=m*s[7:8]; fy=s[8:9]
        lo=(mx*(1.0-fy)).astype(bf16); hi=(mx*fy).astype(bf16)
        d=depth_table(iz,cz,s[9:10],kc)
        a=plane_rows(iy,cy,lo,hi)
        e=jnp.where(cy.astype(i16)==127,hi,jnp.zeros_like(hi))
        zz=jnp.zeros_like(it).astype(bf16)
        l=jnp.concatenate([a,jnp.where(it==0,e,zz)],0)
        u=lax.dot_general(l,d,nt,preferred_element_type=f32)
        grid[0]+=u[0:128]; rim[...]+=u[128:136]
        return 0
    lax.fori_loop(0,n//kc,body,0)

V=pl.BlockSpec(memory_space=pltpu.VMEM)
def deposit_own(st,kc=512,name="dep_own"):
    return pl.pallas_call(functools.partial(deposit_own_kernel,kc),
        out_shape=[jax.ShapeDtypeStruct((2,128,MZ),f32),jax.ShapeDtypeStruct((8,MZ),f32)],
        in_specs=[V],out_specs=[V,V],
        compiler_params=pltpu.CompilerParams(vmem_limit_bytes=48<<20),name=name)(st)
def deposit_in(st,g,r,kc=512,name="dep_in"):
    return pl.pallas_call(functools.partial(deposit_in_kernel,kc),
        out_shape=[jax.ShapeDtypeStruct((2,128,MZ),f32),jax.ShapeDtypeStruct((8,MZ),f32)],
        in_specs=[V,V,V],out_specs=[V,V],
        compiler_params=pltpu.CompilerParams(vmem_limit_bytes=48<<20),name=name)(st,g,r)


def on_device(positions, mass, smooth, cell_y, cell_z, cic_frac, pair_blocks, pair_count):
    half = mass.shape[0] // 2
    hb = pair_blocks.shape[0] // 2
    state = jnp.concatenate(
        [positions, mass[None], smooth[None], cell_y.astype(f32)[None], cell_z.astype(f32)[None], cic_frac], axis=0
    )
    slabs = lax.axis_size("slab")
    cols = lax.axis_size("col")
    up = [(i, (i + 1) % slabs) for i in range(slabs)]
    down = [((i + 1) % slabs, i) for i in range(slabs)]
    right = [(i, (i + 1) % cols) for i in range(cols)]
    lo = lax.ppermute(state[:, half:], "slab", up)
    hi = lax.ppermute(state[:5, :half], "slab", down)
    grid, rim = deposit_own(state, 1024)
    den, term = density(state, lo, hi, pair_blocks, pair_count, 32)
    tlo = lax.ppermute(term[hb:], "slab", up)
    thi = lax.ppermute(term[:hb], "slab", down)
    grid, rim = deposit_in(lo, grid, rim, 1024)
    rows = lax.ppermute(rim[:2], "col", right)
    acc = force(state, lo, hi, term, tlo, thi, pair_blocks, pair_count, 16)
    grid = grid.at[:, 0].add(rows)
    return den.reshape(-1), acc, grid


def solution(mesh):
    return jax.shard_map(
        on_device,
        mesh=mesh,
        in_specs=(
            P(None, ("slab", "col")),
            P(("slab", "col")),
            P(("slab", "col")),
            P(("slab", "col")),
            P(("slab", "col")),
            P(None, ("slab", "col")),
            P(("slab", "col"), None),
            P(("slab", "col")),
        ),
        out_specs=(P(("slab", "col")), P(None, ("slab", "col")), P("slab", "col", None)),
        check_vma=False,
    )
```

time: 268 us -> 85.2 us (0.32); the launches traced: 264 us -> 84.6 us
  other arithmetic: 123 us -> 1.61 us
  local copies, waits for them, and re-layouts: 75.1 us -> 6.66 us
  Pallas kernels: 0 us -> 49.3 us
  matrix products: 32.1 us -> 0 us
  starting transfers between devices: 29.8 us -> 23.1 us
    reduce_sum x32 -> x0, other arithmetic: 70.7 us -> none  [the longest x16 48.4 us: block_force(): jnp.sum(factor * separation, axis=(2, 3))]
    pallas_call x0 -> x4, Pallas kernels: none -> 49.3 us  [the longest x1 24.7 us: force(): pl.pallas_call(functools.partial(force_kernel, G), out_shape=jax.ShapeDty...]
    dot_general x16 -> x0, matrix products: 32.1 us -> none  [accumulate(): lax.dot_general(loads, depth, (((0,), (0,)), ((), ())), preferred_element...]
    gather x96 -> x0, local copies, waits for them, and re-layouts: 29 us -> none  [the longest x32 9.89 us: force_step(): ext_blocks[:, partner_ids]]
    sub x48 -> x0, other arithmetic: 22.4 us -> none  [the longest x32 11.3 us: block_force(): own_rows[component][:, :, None, None]]
    select_n x49 -> x0, other arithmetic: 21.8 us -> none  [the longest x16 10.8 us: density_step(): return block_density(own_rows, ext_blocks[:, partner_ids], slot_keep)]
    mul x32 -> x0, local copies, waits for them, and re-layouts: 21.4 us -> none  [the longest x16 10.7 us: block_force(): weights = partner_rows[3] * slot_keep[:, :, None]]
    slice x23 -> x3, local copies, waits for them, and re-layouts: 15.1 us -> 0.03 us  [the longest x1 0.02 us: on_device(): lo = lax.ppermute(state[:, half:], 'slab', up)]
  transfers between devices with their start and end apart: 6 -> 5, of which waited for: 1 -> 1; matrix products, arithmetic and copies ran while one was open for 85% -> 4% of each run, Pallas kernels for 0% -> 29%
where the time goes in v1:
time: 85.2 us; the launch traced here: 84.6 us
  Pallas kernels  49.3 us (58%)
  starting transfers between devices  23.1 us (27%)
  local copies, waits for them, and re-layouts  6.66 us (8%)
  waiting for transfers between devices  3.06 us (4%)
  other arithmetic  1.61 us (2%)
    pallas_call x1, Pallas kernels, force(): pl.pallas_call(functools.partial(force_kernel, G), out_shape=jax.ShapeDty...  24.7 us
    pallas_call x1, Pallas kernels, density(): pl.pallas_call(functools.partial(density_kernel, G), out_shape=[jax.Shape...  13.4 us
    ppermute x1, starting transfers between devices, on_device(): hi = lax.ppermute(state[:5, :half], 'slab', down)  13.3 us
    pallas_call x1, Pallas kernels, deposit_own(): pl.pallas_call(functools.partial(deposit_own_kernel, kc), out_shape=[jax....  6.75 us
    pallas_call x1, Pallas kernels, deposit_in(): pl.pallas_call(functools.partial(deposit_in_kernel, kc), out_shape=[jax.S...  4.45 us
    ppermute x1, starting transfers between devices, on_device(): rows = lax.ppermute(rim[:2], 'col', right)  3.59 us
    ppermute x1, waiting for transfers between devices, on_device(): tlo = lax.ppermute(term[hb:], 'slab', up)  3.05 us
    concatenate x1, local copies, waits for them, and re-layouts, on_device(): jnp.concatenate([positions, mass[None], smooth[None], cell_y.astype(f32)[...  2.96 us
  transfers between devices with their start and end apart: 5, of which 1 were waited for; matrix products, arithmetic and copies ran while one was open for 4% of the time, Pallas kernels for 29%

profile of v1, /device:TPU:8, one launch (start us, length us, event | category | flops | bytes accessed | tf_op | source)
XLA Modules:
  0.0 84.6 jit_solution(15510870785129291596)
XLA Ops:
  0.6 0.0 copy-start.1
  0.6 0.8 convert_element_type.6
  1.4 0.8 convert_element_type.7
  2.2 0.0 copy-done.1
  2.2 3.0 %concatenate.8.own.st = f32[10,8192]{1,0:T(8,128)S(1)} concatenate(f32[3,8192]{1,0:T(4,128)S(1)} %copy-done.1, f32[1,8192]{1,0:T(1,128)} %bitcast.7, f32[1,8192]{1,0:T(1,128)} %bitcast.9, f32[1,8192]{1,0:T(1,128)S(1)} %bitcast.11, f32[1,8192]{1,0:T(1,128)S(1)} %bitcast.12, f32[3,8192]{1,0:T(4,128)} %param.15), dimensions={0} | concatenate | bytes 655360 | tf_op jit(solution)/shard_map/concatenate | solution.py:248
  5.2 0.0 copy-start.2
  5.2 0.0 copy-start.3
  5.2 1.9 %collective-permute-start = (f32[10,4096]{1,0:T(8,128)S(1)}, f32[10,4096]{1,0:T(8,128)S(1)}, u32[]{:S(2)}, u32[]{:S(2)}) collective-permute-start(f32[10,4096]{1,0:T(8,128)S(1)} %slice.44), channel_id=1, source_target_pairs={{0,8},{8,16},{16,24},{24,32},{32,40},{40,48},{48,56},{56,64},{64,7... | collective-permute-start | bytes 491528 | tf_op jit(solution)/shard_map/ppermute | solution.py:256
  7.2 0.0 copy-done.2
  7.2 0.0 copy-done.3
  7.2 0.0 copy-start.4
  7.2 13.3 %collective-permute-start.1 = (f32[5,4096]{1,0:T(8,128)S(1)}, f32[5,4096]{1,0:T(8,128)S(1)}, u32[]{:S(2)}, u32[]{:S(2)}) collective-permute-start(f32[5,4096]{1,0:T(8,128)S(1)} %pad_maximum_fusion), channel_id=1, source_target_pairs={{8,0},{16,8},{24,16},{32,24},{40,32},{48,40},{56,48},{64,56},{72,6... | collective-permute-start | bytes 245768 | tf_op jit(solution)/shard_map/ppermute | solution.py:257
  20.5 6.8 %dep_own.1 = (f32[2,128,1024]{2,1,0:T(8,128)S(1)}, f32[8,1024]{1,0:T(8,128)S(1)}) custom-call(f32[10,8192]{1,0:T(8,128)S(1)} %concatenate.8.own.st), custom_call_target="tpu_custom_call" | custom-call | tf_op jit(solution)/shard_map/dep_own/pallas_call | solution.py:234
  27.3 0.0 copy-done.4
  27.3 0.1 copy.11.pb
  27.4 0.0 collective-permute-done.lo.st
  27.4 4.5 %dep_in.1 = (f32[2,128,1024]{2,1,0:T(8,128)}, f32[8,1024]{1,0:T(8,128)S(1)}) custom-call(f32[10,4096]{1,0:T(8,128)S(1)} %collective-permute-done.lo.st, f32[2,128,1024]{2,1,0:T(8,128)S(1)} %get-tuple-element.23.g_in, f32[8,1024]{1,0:T(8,128)S(1)} %get-tuple-element.24.r_in), custom_call_target="tpu_custom_call" | custom-call | tf_op jit(solution)/shard_map/dep_in/pallas_call | solution.py:239
  31.9 0.0 copy-start
  31.9 3.6 %collective-permute-start.4 = (f32[2,1024]{1,0:T(2,128)S(1)}, f32[2,1024]{1,0:T(2,128)S(1)}, u32[]{:S(2)}, u32[]{:S(2)}) collective-permute-start(f32[2,1024]{1,0:T(2,128)S(1)} %slice.43), channel_id=1, source_target_pairs={{0,1},{1,2},{2,3},{3,4},{4,5},{5,6},{6,7},{7,0},{8,9},{9,10},{10,1... | collective-permute-start | bytes 24584 | tf_op jit(solution)/shard_map/ppermute | solution.py:263
  35.5 0.0 collective-permute-done.1.hi
  35.5 0.0 copy-done
  35.5 13.4 %density.1 = (f32[64,128]{1,0:T(8,128)}, f32[64,128]{1,0:T(8,128)S(1)}) custom-call(f32[10,8192]{1,0:T(8,128)S(1)} %concatenate.8.own.st, f32[10,4096]{1,0:T(8,128)S(1)} %collective-permute-done.lo.st, f32[5,4096]{1,0:T(8,128)S(1)} %collective-permute-done.1.hi, s32[64,9]{1,0:T(8,128)S(1)} %copy.11.pb, s32[64]{0:T(128)S(1)} %copy-done), custom_call_target="tpu_custom_call" | custom-call | tf_op jit(solution)/shard_map/density/pallas_call | solution.py:83
  48.9 2.3 %collective-permute-start.3 = (f32[32,128]{1,0:T(8,128)S(1)}, f32[32,128]{1,0:T(8,128)S(1)}, u32[]{:S(2)}, u32[]{:S(2)}) collective-permute-start(f32[32,128]{1,0:T(8,128)S(1)} %get-tuple-element.27), channel_id=1, source_target_pairs={{8,0},{16,8},{24,16},{32,24},{40,32},{48,40},{56,48},{64,56},{72,6... | collective-permute-start | bytes 49160 | tf_op jit(solution)/shard_map/ppermute | solution.py:261
  51.2 2.0 %collective-permute-start.2 = (f32[32,128]{1,0:T(8,128)S(1)}, f32[32,128]{1,0:T(8,128)S(1)}, u32[]{:S(2)}, u32[]{:S(2)}) collective-permute-start(f32[32,128]{1,0:T(8,128)S(1)} %get-tuple-element.28), channel_id=1, source_target_pairs={{0,8},{8,16},{16,24},{24,32},{32,40},{40,48},{48,56},{56,64},{64,7... | collective-permute-start | bytes 49160 | tf_op jit(solution)/shard_map/ppermute | solution.py:260
  53.2 2.0 %copy.13 = f32[2,128,1024]{2,0,1:T(2,128)S(1)} copy(f32[2,128,1024]{2,1,0:T(8,128)} %get-tuple-element.25) | data formatting | bytes 2097152 | tf_op jit(solution)/shard_map/dep_in/pallas_call | solution.py:239
  55.2 0.0 collective-permute-done.4
  55.3 1.5 %scatter-add.4 = f32[2,128,1024]{2,1,0:T(8,128)} dynamic-update-slice(f32[2,128,1024]{2,1,0:T(8,128)} %get-tuple-element.25, f32[2,1,1024]{2,1,0:T(1,128)S(1)} %copy.14, s32[]{:T(128)} %constant.26.clone.1, s32[]{:T(128)} %constant.26.clone.1, s32[]{:T(128)} %constant.26.clone.1) | dynamic-update-slice | bytes 16388 | tf_op jit(solution)/shard_map/scatter-add | solution.py:265
  56.8 0.0 collective-permute-done.3.thi
  56.8 3.0 %collective-permute-done.2.tlo = f32[32,128]{1,0:T(8,128)S(1)} collective-permute-done((f32[32,128]{1,0:T(8,128)S(1)}, f32[32,128]{1,0:T(8,128)S(1)}, u32[]{:S(2)}, u32[]{:S(2)}) %collective-permute-start.2) | collective-permute-done | bytes 16416 | tf_op jit(solution)/shard_map/ppermute | solution.py:260
  59.8 24.7 %force.1 = f32[3,8192]{1,0:T(4,128)} custom-call(f32[10,8192]{1,0:T(8,128)S(1)} %concatenate.8.own.st, f32[10,4096]{1,0:T(8,128)S(1)} %collective-permute-done.lo.st, f32[5,4096]{1,0:T(8,128)S(1)} %collective-permute-done.1.hi, f32[64,128]{1,0:T(8,128)S(1)} %get-tuple-element.22.town, f32[32,128]{1,0:T(8,128)S(1)} %collective-permute-done.2.tlo, ...), custom_call_target="tpu_custom_call" | custom-call | tf_op jit(solution)/shard_map/force/pallas_call | solution.py:150
  (6 shorter events, 0.1 us)
Async XLA Ops:
  0.6 1.6 %copy-start.1 = (f32[3,8192]{1,0:T(4,128)S(1)}, f32[3,8192]{1,0:T(4,128)}, u32[]{:S(2)}) copy-start(f32[3,8192]{1,0:T(4,128)} %param.10) | copy-start | bytes 294916
  5.2 2.0 %copy-start.2 = (f32[8192]{0:T(1024)S(1)}, f32[8192]{0:T(1024)}, u32[]{:S(2)}) copy-start(f32[8192]{0:T(1024)} %param.11) | copy-start | bytes 98308
  5.2 2.0 %copy-start.3 = (f32[8192]{0:T(1024)S(1)}, f32[8192]{0:T(1024)}, u32[]{:S(2)}) copy-start(f32[8192]{0:T(1024)} %param.12) | copy-start | bytes 98308
  5.2 22.2 %collective-permute-start = (f32[10,4096]{1,0:T(8,128)S(1)}, f32[10,4096]{1,0:T(8,128)S(1)}, u32[]{:S(2)}, u32[]{:S(2)}) collective-permute-start(f32[10,4096]{1,0:T(8,128)S(1)} %slice.44), channel_id=1, source_target_pairs={{0,8},{8,16},{16,24},{24,32},{32,40},{40,48},{48,56},{56,64},{64,7... | collective-permute-start | bytes 491528 | tf_op jit(solution)/shard_map/ppermute | solution.py:256
  7.2 20.1 %copy-start.4 = (s32[64,9]{0,1:T(8,128)S(1)}, s32[64,9]{0,1:T(8,128)}, u32[]{:S(2)}) copy-start(s32[64,9]{0,1:T(8,128)} %param.16) | copy-start | bytes 6916
  7.2 28.2 %collective-permute-start.1 = (f32[5,4096]{1,0:T(8,128)S(1)}, f32[5,4096]{1,0:T(8,128)S(1)}, u32[]{:S(2)}, u32[]{:S(2)}) collective-permute-start(f32[5,4096]{1,0:T(8,128)S(1)} %pad_maximum_fusion), channel_id=1, source_target_pairs={{8,0},{16,8},{24,16},{32,24},{40,32},{48,40},{56,48},{64,56},{72,6... | collective-permute-start | bytes 245768 | tf_op jit(solution)/shard_map/ppermute | solution.py:257
  31.9 3.6 %copy-start = (s32[64]{0:T(128)S(1)}, s32[64]{0:T(128)}, u32[]{:S(2)}) copy-start(s32[64]{0:T(128)} %pc.3) | copy-start | bytes 772
  31.9 23.4 %collective-permute-start.4 = (f32[2,1024]{1,0:T(2,128)S(1)}, f32[2,1024]{1,0:T(2,128)S(1)}, u32[]{:S(2)}, u32[]{:S(2)}) collective-permute-start(f32[2,1024]{1,0:T(2,128)S(1)} %slice.43), channel_id=1, source_target_pairs={{0,1},{1,2},{2,3},{3,4},{4,5},{5,6},{6,7},{7,0},{8,9},{9,10},{10,1... | collective-permute-start | bytes 24584 | tf_op jit(solution)/shard_map/ppermute | solution.py:263
  48.9 7.9 %collective-permute-start.3 = (f32[32,128]{1,0:T(8,128)S(1)}, f32[32,128]{1,0:T(8,128)S(1)}, u32[]{:S(2)}, u32[]{:S(2)}) collective-permute-start(f32[32,128]{1,0:T(8,128)S(1)} %get-tuple-element.27), channel_id=1, source_target_pairs={{8,0},{16,8},{24,16},{32,24},{40,32},{48,40},{56,48},{64,56},{72,6... | collective-permute-start | bytes 49160 | tf_op jit(solution)/shard_map/ppermute | solution.py:261
  51.2 8.7 %collective-permute-start.2 = (f32[32,128]{1,0:T(8,128)S(1)}, f32[32,128]{1,0:T(8,128)S(1)}, u32[]{:S(2)}, u32[]{:S(2)}) collective-permute-start(f32[32,128]{1,0:T(8,128)S(1)} %get-tuple-element.28), channel_id=1, source_target_pairs={{0,8},{8,16},{16,24},{24,32},{32,40},{40,48},{48,56},{56,64},{64,7... | collective-permute-start | bytes 49160 | tf_op jit(solution)/shard_map/ppermute | solution.py:260

commit v2 on v0

v2 whole, which is shorter than its diff:
```python
import functools

import jax
import jax.numpy as jnp
from jax import lax
from jax.experimental import pallas as pl
from jax.experimental.pallas import tpu as pltpu
from jax.sharding import PartitionSpec as P

BLK = 128
NP = 9
XP = 2
MYD = 128
MZ = 1024
LOG2E = 1.4426950408889634
KF = 48
GROUP = 32
SPAN = 1024

f32 = jnp.float32
bf16 = jnp.bfloat16
i16 = jnp.int16
i32 = jnp.int32

VM = pl.BlockSpec(memory_space=pltpu.VMEM)
SM = pl.BlockSpec(memory_space=pltpu.SMEM)
AN = pl.BlockSpec(memory_space=pl.ANY)
HB = pl.BlockSpec(memory_space=pltpu.HBM)
NT = (((1,), (1,)), ((), ()))


def lanes(i, width=BLK):
    return pl.ds(pl.multiple_of(i * width, BLK), width)


def pack_kernel(pos, mass, smooth, cy, cz, frac, pairs, counts, own, tail, head, vpairs, vcounts, vpos, vmass, vsmooth, vcy, vcz, vfrac, sems):
    half = own.shape[1] // 2
    moves = (
        (pos, vpos),
        (mass, vmass),
        (smooth, vsmooth),
        (cy, vcy),
        (cz, vcz),
        (frac, vfrac),
        (pairs, vpairs),
        (counts, vcounts),
    )
    copies = [pltpu.make_async_copy(src, dst, sems.at[k]) for k, (src, dst) in enumerate(moves)]
    for copy in copies:
        copy.start()
    for copy in copies:
        copy.wait()
    own[0:3] = vpos[...]
    own[3:4] = vmass[...]
    own[4:5] = vsmooth[...]
    own[5:6] = vcy[...].astype(f32)
    own[6:7] = vcz[...].astype(f32)
    own[7:10] = vfrac[...]
    tail[...] = own[:, half:]
    head[...] = own[0:5, :half]


def pack(positions, mass, smooth, cell_y, cell_z, cic_frac, pairs, counts):
    n = mass.shape[0]
    nb = counts.shape[0]
    return pl.pallas_call(
        pack_kernel,
        out_shape=[
            jax.ShapeDtypeStruct((10, n), f32),
            jax.ShapeDtypeStruct((10, n // 2), f32),
            jax.ShapeDtypeStruct((5, n // 2), f32),
            jax.ShapeDtypeStruct((NP, nb), i32),
            jax.ShapeDtypeStruct((1, nb), i32),
        ],
        in_specs=[HB] * 8,
        out_specs=[VM] * 5,
        scratch_shapes=[
            pltpu.VMEM((3, n), f32),
            pltpu.VMEM((1, n), f32),
            pltpu.VMEM((1, n), f32),
            pltpu.VMEM((1, n), i32),
            pltpu.VMEM((1, n), i32),
            pltpu.VMEM((3, n), f32),
            pltpu.SemaphoreType.DMA((8,)),
        ],
        name="pack",
    )(positions, mass[None], smooth[None], cell_y[None], cell_z[None], cic_frac, pairs, counts[None])


def split3(x):
    h = x.astype(bf16).astype(f32)
    r = x - h
    m = r.astype(bf16).astype(f32)
    return h, m, r - m


def stack_a(x):
    h, m, l = split3(x)
    return jnp.concatenate([h, h, m, m, h, l], 0).astype(bf16)


def stack_b(x):
    h, m, l = split3(x)
    return jnp.concatenate([h, m, h, m, l, h], 0).astype(bf16)


def norm_sq(x):
    return x[0:1] * x[0:1] + x[1:2] * x[1:2] + x[2:3] * x[2:3]


def partner_tile(st):
    x, m, s = st[0:3], st[3:4], st[4:5]
    one = jnp.ones_like(m)
    rows = jnp.concatenate([x, norm_sq(x), jnp.log2(m), 0.5 * s * s, one, jnp.zeros_like(one)], 0)
    return stack_a(rows).T


def fill_partners(src, a_ref, at, count):
    step = min(16, count)

    def body(i, _):
        for u in range(step):
            b = i * step + u
            a_ref[at + b] = partner_tile(src[0:5, lanes(b)])
        return 0

    lax.fori_loop(0, count // step, body, 0)


def depth_table(iz, cz, fz):
    lo = cz.astype(i16)
    hi = ((cz + 1) & (MZ - 1)).astype(i16)
    w1 = fz.astype(bf16)
    w0 = (1.0 - fz).astype(bf16)
    return jnp.where(iz == lo, w0, jnp.where(iz == hi, w1, jnp.zeros_like(w1)))


def row_table(iy, cy, mx, fy):
    lo = (mx * (1.0 - fy)).astype(bf16)
    hi = (mx * fy).astype(bf16)
    zero = jnp.zeros_like(hi)
    main = jnp.where(iy == cy.astype(i16), lo, jnp.where(iy == (cy + 1).astype(i16), hi, zero))
    return main, jnp.where(cy.astype(i16) == MYD - 1, hi, zero)


def cell_rows(st, at, span):
    s = st[:, pl.ds(pl.multiple_of(at, BLK), span)]
    return s[3:4], s[5:6].astype(i32), s[6:7].astype(i32), s[7:8], s[8:9], s[9:10]


def deposit_own_kernel(st, pb, pc, grid, rim, a_own, lst, total):
    n = st.shape[1]
    half = n // 2
    nb = pc.shape[1]
    fill_partners(st, a_own, 0, nb)
    iz = lax.broadcasted_iota(i16, (MZ, SPAN), 0)
    iy = lax.broadcasted_iota(i16, (MYD, SPAN), 0)
    ir = lax.broadcasted_iota(i16, (16, SPAN), 0)
    zero = jnp.zeros((16, SPAN), bf16)

    def listed(b, pos):
        for k in range(NP):
            lst[pos + k] = pb[k, b] + b * 256
        return pos + pc[0, b]

    count = lax.fori_loop(0, nb, listed, i32(0), unroll=8)
    for k in range(GROUP):
        lst[count + k] = i32(nb * 256)
    total[0] = (count + GROUP - 1) // GROUP
    grid[...] = jnp.zeros_like(grid)
    rim[...] = jnp.zeros_like(rim)

    def first(i, _):
        m, cy, cz, fx, fy, fz = cell_rows(st, i * SPAN, SPAN)
        main0, edge0 = row_table(iy, cy, m * (1.0 - fx), fy)
        main1, edge1 = row_table(iy, cy, m * fx, fy)
        edge = jnp.where(ir == 0, edge0, jnp.where(ir == 1, edge1, zero))
        u = lax.dot_general(
            jnp.concatenate([main0, main1, edge], 0), depth_table(iz, cz, fz), NT, preferred_element_type=f32
        )
        grid[0] += u[0:MYD]
        grid[1] += u[MYD : 2 * MYD]
        rim[...] += u[2 * MYD : 2 * MYD + 8]
        return 0

    lax.fori_loop(0, half // SPAN, first, 0)

    def second(i, _):
        m, cy, cz, fx, fy, fz = cell_rows(st, half + i * SPAN, SPAN)
        main, edge = row_table(iy, cy, m * (1.0 - fx), fy)
        u = lax.dot_general(
            jnp.concatenate([main, jnp.where(ir == 1, edge, zero)], 0),
            depth_table(iz, cz, fz),
            NT,
            preferred_element_type=f32,
        )
        grid[1] += u[0:MYD]
        rim[...] += u[MYD : MYD + 8]
        return 0

    lax.fori_loop(0, half // SPAN, second, 0)


def deposit_own(st, pb, pc):
    nb = pc.shape[1]
    return pl.pallas_call(
        deposit_own_kernel,
        out_shape=[
            jax.ShapeDtypeStruct((XP, MYD, MZ), f32),
            jax.ShapeDtypeStruct((8, MZ), f32),
            jax.ShapeDtypeStruct((nb, BLK, KF), bf16),
            jax.ShapeDtypeStruct((nb * NP + NP + 2 * GROUP,), i32),
            jax.ShapeDtypeStruct((1,), i32),
        ],
        in_specs=[VM, SM, SM],
        out_specs=[VM, VM, VM, SM, SM],
        compiler_params=pltpu.CompilerParams(vmem_limit_bytes=16 << 20),
        cost_estimate=pl.CostEstimate(flops=4 * st.shape[1] * MYD * MZ, bytes_accessed=4 << 20, transcendentals=0),
        name="deposit_own",
    )(st, pb, pc)


def deposit_in_kernel(st, g_in, r_in, after, grid, rim, edge_row):
    n = st.shape[1]
    iz = lax.broadcasted_iota(i16, (MZ, SPAN), 0)
    iy = lax.broadcasted_iota(i16, (MYD, SPAN), 0)
    ir = lax.broadcasted_iota(i16, (16, SPAN), 0)
    zero = jnp.zeros((16, SPAN), bf16)
    grid[...] = g_in[...]
    rim[...] = r_in[...]

    def body(i, _):
        m, cy, cz, fx, fy, fz = cell_rows(st, i * SPAN, SPAN)
        main, edge = row_table(iy, cy, m * fx, fy)
        u = lax.dot_general(
            jnp.concatenate([main, jnp.where(ir == 0, edge, zero)], 0),
            depth_table(iz, cz, fz),
            NT,
            preferred_element_type=f32,
        )
        grid[0] += u[0:MYD]
        rim[...] += u[MYD : MYD + 8]
        return 0

    lax.fori_loop(0, n // SPAN, body, 0)
    edge_row[...] = grid[:, 0:1, :]


def deposit_in(st, g, r, after):
    return pl.pallas_call(
        deposit_in_kernel,
        out_shape=[
            jax.ShapeDtypeStruct((XP, MYD, MZ), f32),
            jax.ShapeDtypeStruct((8, MZ), f32),
            jax.ShapeDtypeStruct((XP, 1, MZ), f32),
        ],
        in_specs=[VM, VM, VM, AN],
        out_specs=[VM] * 3,
        compiler_params=pltpu.CompilerParams(vmem_limit_bytes=16 << 20),
        cost_estimate=pl.CostEstimate(flops=2 * st.shape[1] * MYD * MZ, bytes_accessed=4 << 20, transcendentals=0),
        name="deposit_in",
    )(st, g, r, after)


def density_kernel(own, lo, hi, a_own, lst, total, den, term, a_ref, b_ref, acc):
    nb = den.shape[0]
    hb = nb // 2
    fill_partners(lo, a_ref, 0, hb)
    fill_partners(hi, a_ref, hb + nb, hb)
    a_ref[hb : hb + nb] = a_own[...]

    def own_tile(i, _):
        st = own[0:5, lanes(i)]
        x, s = st[0:3], st[4:5]
        one = jnp.ones_like(s)
        zero = jnp.zeros_like(s)
        c = LOG2E / (s * s)
        b_ref[i] = stack_b(jnp.concatenate([2.0 * c * x, -c, one, zero, -c * norm_sq(x), zero], 0))
        return 0

    lax.fori_loop(0, nb, own_tile, 0, unroll=4)
    b_ref[nb] = jnp.zeros((KF, BLK), bf16)
    acc[...] = jnp.zeros_like(acc)

    def main(it, _):
        for g in range(GROUP):
            code = lst[it * GROUP + g]
            e = jnp.dot(a_ref[code & 255], b_ref[code >> 8], preferred_element_type=f32)
            acc[code >> 8] += jnp.exp2(e).reshape(BLK // 8, 8, BLK).sum(0)
        return 0

    lax.fori_loop(0, total[0], main, 0)
    d = acc[0:nb].sum(1) * (1.0 / (NP * BLK))
    den[...] = d
    term[...] = jnp.exp2(jnp.log2(d) * (-1.0 / 3.0))


def density(own, lo, hi, a_own, lst, total):
    nb = a_own.shape[0]
    return pl.pallas_call(
        density_kernel,
        out_shape=[
            jax.ShapeDtypeStruct((nb, BLK), f32),
            jax.ShapeDtypeStruct((nb, BLK), f32),
            jax.ShapeDtypeStruct((2 * nb, BLK, KF), bf16),
        ],
        in_specs=[VM, VM, VM, VM, SM, SM],
        out_specs=[VM] * 3,
        scratch_shapes=[pltpu.VMEM((nb + 1, KF, BLK), bf16), pltpu.VMEM((nb + 1, 8, BLK), f32)],
        compiler_params=pltpu.CompilerParams(vmem_limit_bytes=16 << 20),
        cost_estimate=pl.CostEstimate(flops=12 * nb * NP * BLK * BLK, bytes_accessed=8 << 20, transcendentals=nb * NP * BLK * BLK),
        name="density",
    )(own, lo, hi, a_own, lst, total)


def force_kernel(own, lo, hi, a_ref, town, tlo, thi, lst, total, out, b_ref, v_ref, acc):
    nb = town.shape[0]
    hb = nb // 2

    def sources(src, t, at, count):
        def body(i, _):
            st = src[0:5, lanes(i)]
            x, m = st[0:3], st[3:4]
            mt = m * t[pl.ds(i, 1), :]
            v = jnp.concatenate([m, m * x, mt, mt * x], 0)
            h = v.astype(bf16).astype(f32)
            v_ref[at + i] = jnp.concatenate([h, v - h], 0).astype(bf16)
            return 0

        lax.fori_loop(0, count, body, 0, unroll=8)

    sources(lo, tlo, 0, hb)
    sources(own, town, hb, nb)
    sources(hi, thi, hb + nb, hb)

    def own_tile(i, _):
        st = own[0:5, lanes(i)]
        x, s = st[0:3], st[4:5]
        one = jnp.ones_like(s)
        z = jnp.zeros_like(s)
        dist = jnp.concatenate([(2.0 * LOG2E) * x, -LOG2E * one, z, z, -LOG2E * norm_sq(x), z], 0)
        spread = jnp.concatenate([z, z, z, z, z, one, 0.5 * s * s, z], 0)
        b_ref[i, :, 0:BLK] = stack_b(dist)
        b_ref[i, :, BLK : 2 * BLK] = stack_b(spread)
        return 0

    lax.fori_loop(0, nb, own_tile, 0, unroll=4)
    b_ref[nb] = jnp.ones((KF, 2 * BLK), bf16)
    acc[...] = jnp.zeros_like(acc)
    lag = 8

    def main(it, _):
        codes = [lst[it * GROUP + g] for g in range(GROUP)]
        forms = {}
        weights = {}
        for step in range(GROUP + 2 * lag):
            if step < GROUP:
                code = codes[step]
                forms[step] = jnp.dot(a_ref[code & 255], b_ref[code >> 8], preferred_element_type=f32)
            g = step - lag
            if 0 <= g < GROUP:
                e = forms.pop(g)
                r = pl.reciprocal(e[:, BLK : 2 * BLK], approx=True)
                weights[g] = (jnp.exp2(e[:, 0:BLK] * r) * r).astype(bf16)
            g = step - 2 * lag
            if 0 <= g < GROUP:
                code = codes[g]
                acc[code >> 8] += jnp.dot(v_ref[code & 255], weights.pop(g), preferred_element_type=f32)
        return 0

    lax.fori_loop(0, total[0], main, 0)

    def finish(i, _):
        a = acc[i]
        s = a[0:8] + a[8:16]
        x = own[0:3, lanes(i)]
        t = town[pl.ds(i, 1), :]
        f = t * (x * s[0:1] - s[1:4]) + (x * s[4:5] - s[5:8])
        out[:, lanes(i)] = f * (2.0 / (NP * BLK))
        return 0

    lax.fori_loop(0, nb, finish, 0, unroll=8)


def force(own, lo, hi, a, town, tlo, thi, lst, total):
    nb = town.shape[0]
    return pl.pallas_call(
        force_kernel,
        out_shape=jax.ShapeDtypeStruct((3, nb * BLK), f32),
        in_specs=[VM] * 7 + [SM, SM],
        out_specs=VM,
        scratch_shapes=[
            pltpu.VMEM((nb + 1, KF, 2 * BLK), bf16),
            pltpu.VMEM((2 * nb, 16, BLK), bf16),
            pltpu.VMEM((nb + 1, 16, BLK), f32),
        ],
        compiler_params=pltpu.CompilerParams(vmem_limit_bytes=16 << 20),
        cost_estimate=pl.CostEstimate(flops=24 * nb * NP * BLK * BLK, bytes_accessed=8 << 20, transcendentals=2 * nb * NP * BLK * BLK),
        name="force",
    )(own, lo, hi, a, town, tlo, thi, lst, total)


def on_device(positions, mass, smooth, cell_y, cell_z, cic_frac, pair_blocks, pair_count):
    hb = pair_blocks.shape[0] // 2
    slabs = lax.axis_size("slab")
    cols = lax.axis_size("col")
    up = [(i, (i + 1) % slabs) for i in range(slabs)]
    down = [((i + 1) % slabs, i) for i in range(slabs)]
    right = [(i, (i + 1) % cols) for i in range(cols)]
    own, tail, head, pairs, counts = pack(
        positions, mass, smooth, cell_y, cell_z, cic_frac, pair_blocks.T, pair_count
    )
    lo = lax.ppermute(tail, "slab", up)
    hi = lax.ppermute(head, "slab", down)
    grid, rim, a_own, lst, total = deposit_own(own, pairs, counts)
    den, term, a = density(own, lo, hi, a_own, lst, total)
    tlo = lax.ppermute(term[hb:], "slab", up)
    thi = lax.ppermute(term[:hb], "slab", down)
    grid, rim, edge_row = deposit_in(lo, grid, rim, term)
    rows = lax.ppermute(rim[:XP], "col", right)
    acceleration = force(own, lo, hi, a, term, tlo, thi, lst, total)
    rows, acceleration = lax.optimization_barrier((rows, acceleration))
    grid = lax.dynamic_update_slice(grid, edge_row + rows[:, None], (0, 0, 0))
    return den.reshape(-1), acceleration, grid


def solution(mesh):
    return jax.shard_map(
        on_device,
        mesh=mesh,
        in_specs=(
            P(None, ("slab", "col")),
            P(("slab", "col")),
            P(("slab", "col")),
            P(("slab", "col")),
            P(("slab", "col")),
            P(None, ("slab", "col")),
            P(("slab", "col"), None),
            P(("slab", "col")),
        ),
        out_specs=(P(("slab", "col")), P(None, ("slab", "col")), P("slab", "col", None)),
        check_vma=False,
    )
```

time: 268 us -> 72.1 us (0.27)
  the two profiles are of different devices: /device:TPU:8 before, /device:TPU:2 now
where the time goes in v2:
time: 72.1 us; the launch traced here: 71.7 us
  Pallas kernels  40.1 us (56%)
  starting transfers between devices  26.9 us (37%)
  local copies, waits for them, and re-layouts  3.91 us (5%)
  between operations  0.75 us (1%)
    pallas_call x1, Pallas kernels, force(): pl.pallas_call(force_kernel, out_shape=jax.ShapeDtypeStruct((3, nb * BLK)...  14.5 us
    ppermute x1, starting transfers between devices, on_device(): hi = lax.ppermute(head, 'slab', down)  12.4 us
    pallas_call x1, Pallas kernels, density(): pl.pallas_call(density_kernel, out_shape=[jax.ShapeDtypeStruct((nb, BLK),...  9.76 us
    pallas_call x1, Pallas kernels, deposit_own(): pl.pallas_call(deposit_own_kernel, out_shape=[jax.ShapeDtypeStruct((XP, M...  9.26 us
    ppermute x1, starting transfers between devices, on_device(): thi = lax.ppermute(term[:hb], 'slab', down)  7.23 us
    pallas_call x1, Pallas kernels, deposit_in(): pl.pallas_call(deposit_in_kernel, out_shape=[jax.ShapeDtypeStruct((XP, MY...  4.46 us
    ppermute x1, starting transfers between devices, on_device(): rows = lax.ppermute(rim[:XP], 'col', right)  3.47 us
    unnamed x8, local copies, waits for them, and re-layouts  2.4 us
  transfers between devices with their start and end apart: 5, of which 0 were waited for; matrix products, arithmetic and copies ran while one was open for 0% of the time, Pallas kernels for 39%

profile of v2, /device:TPU:2, one launch (start us, length us, event | category | flops | bytes accessed | tf_op | source)
XLA Modules:
  0.0 71.7 jit_solution(3738042683345427723)
XLA Ops:
  0.6 2.1 %pack.1 = (f32[10,8192]{1,0:T(8,128)}, f32[10,4096]{1,0:T(8,128)}, f32[5,4096]{1,0:T(8,128)}, s32[9,64]{1,0:T(8,128)}, s32[1,64]{1,0:T(1,128)}) custom-call(f32[3,8192]{1,0:T(4,128)} %pos.1, f32[1,8192]{1,0:T(1,128)} %bitcast.7, f32[1,8192]{1,0:T(1,128)} %bitcast.8, s32[1,8192]{1,0:T(1,128)} %bitcast.9, s32[1,8192]{1,0:T(1,128)} %bitcast.10, ...), custom_call_target="tpu_custom_call" | custom-call | tf_op jit(solution)/shard_map/pack/pallas_call | solution.py:66
  2.7 12.4 %collective-permute-start.1 = (f32[5,4096]{1,0:T(8,128)}, f32[5,4096]{1,0:T(8,128)S(1)}, u32[]{:S(2)}, u32[]{:S(2)}) collective-permute-start(f32[5,4096]{1,0:T(8,128)} %get-tuple-element.23), channel_id=1, source_target_pairs={{8,0},{16,8},{24,16},{32,24},{40,32},{48,40},{56,48},{64,56},{72,6... | collective-permute-start | bytes 245768 | tf_op jit(solution)/shard_map/ppermute | solution.py:414
  15.1 1.9 %collective-permute-start = (f32[10,4096]{1,0:T(8,128)}, f32[10,4096]{1,0:T(8,128)S(1)}, u32[]{:S(2)}, u32[]{:S(2)}) collective-permute-start(f32[10,4096]{1,0:T(8,128)} %get-tuple-element.22), channel_id=1, source_target_pairs={{0,8},{8,16},{16,24},{24,32},{32,40},{40,48},{48,56},{56,64},{64,7... | collective-permute-start | bytes 491528 | tf_op jit(solution)/shard_map/ppermute | solution.py:413
  17.1 0.0 copy-start
  17.1 1.0 %copy-done = f32[10,8192]{1,0:T(8,128)S(1)} copy-done((f32[10,8192]{1,0:T(8,128)S(1)}, f32[10,8192]{1,0:T(8,128)}, u32[]{:S(2)}) %copy-start) | copy-done | bytes 327704
  18.1 0.0 copy-start.2
  18.1 0.7 copy-done.2
  18.8 0.0 copy-start.3
  18.8 0.7 copy-done.3
  19.5 9.3 %deposit_own.1 = (f32[2,128,1024]{2,1,0:T(8,128)S(1)}, f32[8,1024]{1,0:T(8,128)S(1)}, bf16[64,128,48]{2,1,0:T(8,128)(2,1)S(1)}, s32[649]{0:T(1024)S(1)}, s32[1]{0:T(128)}) custom-call(f32[10,8192]{1,0:T(8,128)S(1)} %copy-done, s32[9,64]{1,0:T(8,128)S(1)} %copy-done.2, s32[1,64]{1,0:T(1,128)S(1)} %copy-done.3), custom_call_target="tpu_custom_call" | custom-call | flops 4294967296 | bytes 4194304 | tf_op jit(solution)/shard_map/deposit_own/pallas_call | solution.py:206
  28.7 0.0 collective-permute-done.1.hi
  28.8 0.0 collective-permute-done.lo.st
  28.8 0.0 copy-start.1
  28.8 9.8 %density.1 = (f32[64,128]{1,0:T(8,128)}, f32[64,128]{1,0:T(8,128)S(1)}, bf16[128,128,48]{2,1,0:T(8,128)(2,1)S(1)}) custom-call(f32[10,8192]{1,0:T(8,128)S(1)} %copy-done, f32[10,4096]{1,0:T(8,128)S(1)} %collective-permute-done.lo.st, f32[5,4096]{1,0:T(8,128)S(1)} %collective-permute-done.1.hi, bf16[64,128,48]{2,1,0:T(8,128)(2,1)S(1)} %get-tuple-element.26.a_own, ...), custom_call_target="tpu_custom_call" | custom-call | flops 113246208 | bytes 8388608 | tf_op jit(solution)/shard_map/density/pallas_call | solution.py:300
  38.5 7.2 %collective-permute-start.4 = (f32[32,128]{1,0:T(8,128)S(1)}, f32[32,128]{1,0:T(8,128)S(1)}, u32[]{:S(2)}, u32[]{:S(2)}) collective-permute-start(f32[32,128]{1,0:T(8,128)S(1)} %get-tuple-element.39), channel_id=1, source_target_pairs={{8,0},{16,8},{24,16},{32,24},{40,32},{48,40},{56,48},{64,56},{72,6... | collective-permute-start | bytes 49160 | tf_op jit(solution)/shard_map/ppermute | solution.py:418
  45.8 1.9 %collective-permute-start.3 = (f32[32,128]{1,0:T(8,128)S(1)}, f32[32,128]{1,0:T(8,128)S(1)}, u32[]{:S(2)}, u32[]{:S(2)}) collective-permute-start(f32[32,128]{1,0:T(8,128)S(1)} %get-tuple-element.40), channel_id=1, source_target_pairs={{0,8},{8,16},{16,24},{24,32},{32,40},{40,48},{48,56},{56,64},{64,7... | collective-permute-start | bytes 49160 | tf_op jit(solution)/shard_map/ppermute | solution.py:417
  47.7 4.5 %deposit_in.1 = (f32[2,128,1024]{2,1,0:T(8,128)}, f32[8,1024]{1,0:T(8,128)S(1)}, f32[2,1,1024]{2,1,0:T(1,128)S(1)}) custom-call(f32[10,4096]{1,0:T(8,128)S(1)} %collective-permute-done.lo.st, f32[2,128,1024]{2,1,0:T(8,128)S(1)} %get-tuple-element.30.g_in, f32[8,1024]{1,0:T(8,128)S(1)} %get-tuple-element.31.r_in, f32[64,128]{1,0:T(8,128)S(1)} %get-tuple-element.32.after.town), custom_call_target="tpu_custom_call" | custom-call | flops 1073741824 | bytes 4194304 | tf_op jit(solution)/shard_map/deposit_in/pallas_call | solution.py:250
  52.2 3.5 %collective-permute-start.2 = (f32[2,1024]{1,0:T(2,128)S(1)}, f32[2,1024]{1,0:T(2,128)S(1)}, u32[]{:S(2)}, u32[]{:S(2)}) collective-permute-start(f32[2,1024]{1,0:T(2,128)S(1)} %slice.9), channel_id=1, source_target_pairs={{0,1},{1,2},{2,3},{3,4},{4,5},{5,6},{6,7},{7,0},{8,9},{9,10},{10,1... | collective-permute-start | bytes 24584 | tf_op jit(solution)/shard_map/ppermute | solution.py:420
  55.6 0.0 collective-permute-done.4.thi
  55.7 0.0 collective-permute-done.3.tlo
  55.7 0.0 copy-done.1
  55.7 14.5 %force.1 = f32[3,8192]{1,0:T(4,128)} custom-call(f32[10,8192]{1,0:T(8,128)S(1)} %copy-done.1, f32[10,4096]{1,0:T(8,128)S(1)} %collective-permute-done.lo.st, f32[5,4096]{1,0:T(8,128)S(1)} %collective-permute-done.1.hi, bf16[128,128,48]{2,1,0:T(8,128)(2,1)S(1)} %get-tuple-element.34.a_ref, f32[64,128]{1,0:T(8,128)S(1)} %get-tuple-element.32.after.town, ...), custom_call_target="tpu_custom_call" | custom-call | flops 226492416 | bytes 8388608 | tf_op jit(solution)/shard_map/force/pallas_call | solution.py:387
  70.2 0.0 collective-permute-done.2
  70.2 1.5 %dynamic_update_slice.3 = f32[2,128,1024]{2,1,0:T(8,128)} dynamic-update-slice(f32[2,128,1024]{2,1,0:T(8,128)} %get-tuple-element.36, f32[2,1,1024]{2,1,0:T(1,128)S(1)} %reshape_add_fusion, s32[]{:T(128)} %constant.0.clone.1, s32[]{:T(128)} %constant.0.clone.1, s32[]{:T(128)} %constant.0.clone.1) | dynamic-update-slice | bytes 16388 | tf_op jit(solution)/shard_map/dynamic_update_slice | solution.py:423
  (3 shorter events, 0.0 us)
Async XLA Ops:
  2.7 26.0 %collective-permute-start.1 = (f32[5,4096]{1,0:T(8,128)}, f32[5,4096]{1,0:T(8,128)S(1)}, u32[]{:S(2)}, u32[]{:S(2)}) collective-permute-start(f32[5,4096]{1,0:T(8,128)} %get-tuple-element.23), channel_id=1, source_target_pairs={{8,0},{16,8},{24,16},{32,24},{40,32},{48,40},{56,48},{64,56},{72,6... | collective-permute-start | bytes 245768 | tf_op jit(solution)/shard_map/ppermute | solution.py:414
  15.1 13.6 %collective-permute-start = (f32[10,4096]{1,0:T(8,128)}, f32[10,4096]{1,0:T(8,128)S(1)}, u32[]{:S(2)}, u32[]{:S(2)}) collective-permute-start(f32[10,4096]{1,0:T(8,128)} %get-tuple-element.22), channel_id=1, source_target_pairs={{0,8},{8,16},{16,24},{24,32},{32,40},{40,48},{48,56},{56,64},{64,7... | collective-permute-start | bytes 491528 | tf_op jit(solution)/shard_map/ppermute | solution.py:413
  17.1 1.0 %copy-start = (f32[10,8192]{1,0:T(8,128)S(1)}, f32[10,8192]{1,0:T(8,128)}, u32[]{:S(2)}) copy-start(f32[10,8192]{1,0:T(8,128)} %get-tuple-element.21.st.own) | copy-start | bytes 983044
  18.1 0.7 copy-start.2
  18.8 0.7 copy-start.3
  28.8 26.9 %copy-start.1 = (f32[10,8192]{1,0:T(8,128)S(1)}, f32[10,8192]{1,0:T(8,128)}, u32[]{:S(2)}) copy-start(f32[10,8192]{1,0:T(8,128)} %get-tuple-element.21.st.own) | copy-start | bytes 983044
  38.5 17.1 %collective-permute-start.4 = (f32[32,128]{1,0:T(8,128)S(1)}, f32[32,128]{1,0:T(8,128)S(1)}, u32[]{:S(2)}, u32[]{:S(2)}) collective-permute-start(f32[32,128]{1,0:T(8,128)S(1)} %get-tuple-element.39), channel_id=1, source_target_pairs={{8,0},{16,8},{24,16},{32,24},{40,32},{48,40},{56,48},{64,56},{72,6... | collective-permute-start | bytes 49160 | tf_op jit(solution)/shard_map/ppermute | solution.py:418
  45.8 9.9 %collective-permute-start.3 = (f32[32,128]{1,0:T(8,128)S(1)}, f32[32,128]{1,0:T(8,128)S(1)}, u32[]{:S(2)}, u32[]{:S(2)}) collective-permute-start(f32[32,128]{1,0:T(8,128)S(1)} %get-tuple-element.40), channel_id=1, source_target_pairs={{0,8},{8,16},{16,24},{24,32},{32,40},{40,48},{48,56},{56,64},{64,7... | collective-permute-start | bytes 49160 | tf_op jit(solution)/shard_map/ppermute | solution.py:417
  52.2 18.0 %collective-permute-start.2 = (f32[2,1024]{1,0:T(2,128)S(1)}, f32[2,1024]{1,0:T(2,128)S(1)}, u32[]{:S(2)}, u32[]{:S(2)}) collective-permute-start(f32[2,1024]{1,0:T(2,128)S(1)} %slice.9), channel_id=1, source_target_pairs={{0,1},{1,2},{2,3},{3,4},{4,5},{5,6},{6,7},{7,0},{8,9},{9,10},{10,1... | collective-permute-start | bytes 24584 | tf_op jit(solution)/shard_map/ppermute | solution.py:420

commit v3 on v2

--- a/solution.py
+++ b/solution.py
@@ -16,6 +16,7 @@
 KF = 48
 GROUP = 32
 SPAN = 1024
+ZB = 512
 
 f32 = jnp.float32
 bf16 = jnp.bfloat16
@@ -33,7 +34,7 @@
     return pl.ds(pl.multiple_of(i * width, BLK), width)
 
 
-def pack_kernel(pos, mass, smooth, cy, cz, frac, pairs, counts, own, tail, head, vpairs, vcounts, vpos, vmass, vsmooth, vcy, vcz, vfrac, sems):
+def pack_kernel(pos, mass, smooth, cy, cz, frac, pairs, counts, own, tail, head, lst, spairs, scounts, vpos, vmass, vsmooth, vcy, vcz, vfrac, sems):
     half = own.shape[1] // 2
     moves = (
         (pos, vpos),
@@ -42,14 +43,23 @@
         (cy, vcy),
         (cz, vcz),
         (frac, vfrac),
-        (pairs, vpairs),
-        (counts, vcounts),
+        (pairs, spairs),
+        (counts, scounts),
     )
     copies = [pltpu.make_async_copy(src, dst, sems.at[k]) for k, (src, dst) in enumerate(moves)]
     for copy in copies:
         copy.start()
-    for copy in copies:
+    for copy in copies[-2:] + copies[:-2]:
         copy.wait()
+    nb = counts.shape[1]
+    at = i32(0)
+    for b in range(nb):
+        for k in range(NP):
+            lst[at + k] = spairs[k, b] + b * 256
+        at = at + scounts[0, b]
+    for k in range(GROUP):
+        lst[at + k] = i32(nb * 256)
+    lst[lst.shape[0] - 1] = (at + GROUP - 1) // GROUP
     own[0:3] = vpos[...]
     own[3:4] = vmass[...]
     own[4:5] = vsmooth[...]
@@ -69,12 +79,13 @@
             jax.ShapeDtypeStruct((10, n), f32),
             jax.ShapeDtypeStruct((10, n // 2), f32),
             jax.ShapeDtypeStruct((5, n // 2), f32),
-            jax.ShapeDtypeStruct((NP, nb), i32),
-            jax.ShapeDtypeStruct((1, nb), i32),
+            jax.ShapeDtypeStruct((nb * NP + NP + 2 * GROUP,), i32),
         ],
         in_specs=[HB] * 8,
-        out_specs=[VM] * 5,
+        out_specs=[VM] * 3 + [SM],
         scratch_shapes=[
+            pltpu.SMEM((NP, nb), i32),
+            pltpu.SMEM((1, nb), i32),
             pltpu.VMEM((3, n), f32),
             pltpu.VMEM((1, n), f32),
             pltpu.VMEM((1, n), f32),
@@ -127,122 +138,109 @@
     lax.fori_loop(0, count // step, body, 0)
 
 
-def depth_table(iz, cz, fz):
-    lo = cz.astype(i16)
-    hi = ((cz + 1) & (MZ - 1)).astype(i16)
-    w1 = fz.astype(bf16)
-    w0 = (1.0 - fz).astype(bf16)
-    return jnp.where(iz == lo, w0, jnp.where(iz == hi, w1, jnp.zeros_like(w1)))
-
-
-def row_table(iy, cy, mx, fy):
-    lo = (mx * (1.0 - fy)).astype(bf16)
-    hi = (mx * fy).astype(bf16)
-    zero = jnp.zeros_like(hi)
-    main = jnp.where(iy == cy.astype(i16), lo, jnp.where(iy == (cy + 1).astype(i16), hi, zero))
-    return main, jnp.where(cy.astype(i16) == MYD - 1, hi, zero)
-
-
-def cell_rows(st, at, span):
-    s = st[:, pl.ds(pl.multiple_of(at, BLK), span)]
-    return s[3:4], s[5:6].astype(i32), s[6:7].astype(i32), s[7:8], s[8:9], s[9:10]
-
-
-def deposit_own_kernel(st, pb, pc, grid, rim, a_own, lst, total):
+def hat_parts(c, low, high, wrap):
+    odd = (c & 1) != 0
+    row = lax.broadcasted_iota(i32, (16, c.shape[1]), 0)
+    even_row = (row & 1) == 0
+    at = jnp.where(even_row, ((c + 1) >> 1) & wrap, c >> 1)
+    value = jnp.where(even_row, jnp.where(odd, high, low), jnp.where(odd, low, high))
+    hit = jnp.where((at & 7) == (row >> 1), value, 0.0)
+    return (at >> 3).astype(f32), hit.astype(bf16)
+
+
+def hat_table(top, hit, tiles):
+    zero = jnp.zeros_like(hit)
+    return jnp.concatenate([jnp.where(top == jnp.full((), t, bf16), hit, zero) for t in range(tiles)], 0)
+
+
+def row_table(cy, mx, fy):
+    high = mx * fy
+    top, hit = hat_parts(cy, mx * (1.0 - fy), high, MYD - 1)
+    edge = jnp.where(cy == MYD - 1, high, 0.0).astype(bf16)
+    return hat_table(top.astype(bf16), hit, MYD // 16), edge
+
+
+def fill_tables(st, at, k, planes, edges, rows_ref, top_ref, hit_ref):
+    span = pl.ds(k * SPAN, SPAN)
+    s = st[:, pl.ds(at + k * SPAN, SPAN)]
+    m, cy, cz, fx, fy, fz = s[3:4], s[5:6].astype(i32), s[6:7].astype(i32), s[7:8], s[8:9], s[9:10]
+    row = lax.broadcasted_iota(i32, (16, SPAN), 0)
+    rim = jnp.zeros((16, SPAN), bf16)
+    for n, (plane, edge_at) in enumerate(zip(planes, edges)):
+        main, edge = row_table(cy, m * (fx if plane else 1.0 - fx), fy)
+        rows_ref[n * MYD : (n + 1) * MYD, span] = main
+        rim = jnp.where(row == edge_at, edge.astype(f32), rim.astype(f32)).astype(bf16)
+    rows_ref[len(planes) * MYD : len(planes) * MYD + 16, span] = rim
+    top, hit = hat_parts(cz, 1.0 - fz, fz, MZ // 2 - 1)
+    top_ref[:, span] = top
+    hit_ref[:, span] = hit
+
+
+def table_scratch(planes, n):
+    return [
+        pltpu.VMEM((planes * MYD + 16, n), bf16),
+        pltpu.VMEM((16, n), f32),
+        pltpu.VMEM((16, n), bf16),
+    ]
+
+
+def deposit_dot(z, rows_ref, top_ref, hit_ref):
+    tiles = ZB // 16
+    top = (top_ref[...] - (z * tiles).astype(f32)).astype(bf16)
+    return lax.dot_general(rows_ref[...], hat_table(top, hit_ref[...], tiles), NT, preferred_element_type=f32)
+
+
+def deposit_own_kernel(st, grid, rim, a_own, rows1, top1, hit1, rows2, top2, hit2):
     n = st.shape[1]
     half = n // 2
-    nb = pc.shape[1]
-    fill_partners(st, a_own, 0, nb)
-    iz = lax.broadcasted_iota(i16, (MZ, SPAN), 0)
-    iy = lax.broadcasted_iota(i16, (MYD, SPAN), 0)
-    ir = lax.broadcasted_iota(i16, (16, SPAN), 0)
-    zero = jnp.zeros((16, SPAN), bf16)
-
-    def listed(b, pos):
-        for k in range(NP):
-            lst[pos + k] = pb[k, b] + b * 256
-        return pos + pc[0, b]
-
-    count = lax.fori_loop(0, nb, listed, i32(0), unroll=8)
-    for k in range(GROUP):
-        lst[count + k] = i32(nb * 256)
-    total[0] = (count + GROUP - 1) // GROUP
-    grid[...] = jnp.zeros_like(grid)
-    rim[...] = jnp.zeros_like(rim)
-
-    def first(i, _):
-        m, cy, cz, fx, fy, fz = cell_rows(st, i * SPAN, SPAN)
-        main0, edge0 = row_table(iy, cy, m * (1.0 - fx), fy)
-        main1, edge1 = row_table(iy, cy, m * fx, fy)
-        edge = jnp.where(ir == 0, edge0, jnp.where(ir == 1, edge1, zero))
-        u = lax.dot_general(
-            jnp.concatenate([main0, main1, edge], 0), depth_table(iz, cz, fz), NT, preferred_element_type=f32
-        )
-        grid[0] += u[0:MYD]
-        grid[1] += u[MYD : 2 * MYD]
-        rim[...] += u[2 * MYD : 2 * MYD + 8]
-        return 0
-
-    lax.fori_loop(0, half // SPAN, first, 0)
-
-    def second(i, _):
-        m, cy, cz, fx, fy, fz = cell_rows(st, half + i * SPAN, SPAN)
-        main, edge = row_table(iy, cy, m * (1.0 - fx), fy)
-        u = lax.dot_general(
-            jnp.concatenate([main, jnp.where(ir == 1, edge, zero)], 0),
-            depth_table(iz, cz, fz),
-            NT,
-            preferred_element_type=f32,
-        )
-        grid[1] += u[0:MYD]
-        rim[...] += u[MYD : MYD + 8]
-        return 0
-
-    lax.fori_loop(0, half // SPAN, second, 0)
-
-
-def deposit_own(st, pb, pc):
-    nb = pc.shape[1]
+    fill_partners(st, a_own, 0, a_own.shape[0])
+    for k in range(half // SPAN):
+        fill_tables(st, 0, k, (0, 1), (0, 1), rows1, top1, hit1)
+        fill_tables(st, half, k, (0,), (1,), rows2, top2, hit2)
+
+    def body(z, _):
+        at = lanes(z, ZB)
+        u = deposit_dot(z, rows1, top1, hit1)
+        v = deposit_dot(z, rows2, top2, hit2)
+        grid[0, :, at] = u[0:MYD]
+        grid[1, :, at] = u[MYD : 2 * MYD] + v[0:MYD]
+        rim[:, at] = u[2 * MYD : 2 * MYD + 8] + v[MYD : MYD + 8]
+        return 0
+
+    lax.fori_loop(0, MZ // ZB, body, 0)
+
+
+def deposit_own(st):
+    nb = st.shape[1] // BLK
     return pl.pallas_call(
         deposit_own_kernel,
         out_shape=[
             jax.ShapeDtypeStruct((XP, MYD, MZ), f32),
             jax.ShapeDtypeStruct((8, MZ), f32),
             jax.ShapeDtypeStruct((nb, BLK, KF), bf16),
-            jax.ShapeDtypeStruct((nb * NP + NP + 2 * GROUP,), i32),
-            jax.ShapeDtypeStruct((1,), i32),
-        ],
-        in_specs=[VM, SM, SM],
-        out_specs=[VM, VM, VM, SM, SM],
+        ],
+        in_specs=[VM],
+        out_specs=[VM] * 3,
+        scratch_shapes=table_scratch(2, st.shape[1] // 2) + table_scratch(1, st.shape[1] // 2),
         compiler_params=pltpu.CompilerParams(vmem_limit_bytes=16 << 20),
         cost_estimate=pl.CostEstimate(flops=4 * st.shape[1] * MYD * MZ, bytes_accessed=4 << 20, transcendentals=0),
         name="deposit_own",
-    )(st, pb, pc)
-
-
-def deposit_in_kernel(st, g_in, r_in, after, grid, rim, edge_row):
-    n = st.shape[1]
-    iz = lax.broadcasted_iota(i16, (MZ, SPAN), 0)
-    iy = lax.broadcasted_iota(i16, (MYD, SPAN), 0)
-    ir = lax.broadcasted_iota(i16, (16, SPAN), 0)
-    zero = jnp.zeros((16, SPAN), bf16)
-    grid[...] = g_in[...]
-    rim[...] = r_in[...]
-
-    def body(i, _):
-        m, cy, cz, fx, fy, fz = cell_rows(st, i * SPAN, SPAN)
-        main, edge = row_table(iy, cy, m * fx, fy)
-        u = lax.dot_general(
-            jnp.concatenate([main, jnp.where(ir == 0, edge, zero)], 0),
-            depth_table(iz, cz, fz),
-            NT,
-            preferred_element_type=f32,
-        )
-        grid[0] += u[0:MYD]
-        rim[...] += u[MYD : MYD + 8]
-        return 0
-
-    lax.fori_loop(0, n // SPAN, body, 0)
+    )(st)
+
+
+def deposit_in_kernel(st, g_in, r_in, after, grid, rim, edge_row, rows, top, hit):
+    for k in range(st.shape[1] // SPAN):
+        fill_tables(st, 0, k, (1,), (0,), rows, top, hit)
+
+    def body(z, _):
+        at = lanes(z, ZB)
+        u = deposit_dot(z, rows, top, hit)
+        grid[0, :, at] = g_in[0, :, at] + u[0:MYD]
+        grid[1, :, at] = g_in[1, :, at]
+        rim[:, at] = r_in[:, at] + u[MYD : MYD + 8]
+        return 0
+
+    lax.fori_loop(0, MZ // ZB, body, 0)
     edge_row[...] = grid[:, 0:1, :]
 
 
@@ -256,15 +254,18 @@
         ],
         in_specs=[VM, VM, VM, AN],
         out_specs=[VM] * 3,
+        scratch_shapes=table_scratch(1, st.shape[1]),
         compiler_params=pltpu.CompilerParams(vmem_limit_bytes=16 << 20),
         cost_estimate=pl.CostEstimate(flops=2 * st.shape[1] * MYD * MZ, bytes_accessed=4 << 20, transcendentals=0),
         name="deposit_in",
     )(st, g, r, after)
 
 
-def density_kernel(own, lo, hi, a_own, lst, total, den, term, a_ref, b_ref, acc):
+def density_kernel(own, lo, hi, a_own, listed, den, term, a_ref, b_ref, acc, lst, sem):
     nb = den.shape[0]
     hb = nb // 2
+    fetch = pltpu.make_async_copy(listed, lst, sem)
+    fetch.start()
     fill_partners(lo, a_ref, 0, hb)
     fill_partners(hi, a_ref, hb + nb, hb)
     a_ref[hb : hb + nb] = a_own[...]
@@ -289,13 +290,14 @@
             acc[code >> 8] += jnp.exp2(e).reshape(BLK // 8, 8, BLK).sum(0)
         return 0
 
-    lax.fori_loop(0, total[0], main, 0)
+    fetch.wait()
+    lax.fori_loop(0, lst[lst.shape[0] - 1], main, 0)
     d = acc[0:nb].sum(1) * (1.0 / (NP * BLK))
     den[...] = d
     term[...] = jnp.exp2(jnp.log2(d) * (-1.0 / 3.0))
 
 
-def density(own, lo, hi, a_own, lst, total):
+def density(own, lo, hi, a_own, lst):
     nb = a_own.shape[0]
     return pl.pallas_call(
         density_kernel,
@@ -304,18 +306,25 @@
             jax.ShapeDtypeStruct((nb, BLK), f32),
             jax.ShapeDtypeStruct((2 * nb, BLK, KF), bf16),
         ],
-        in_specs=[VM, VM, VM, VM, SM, SM],
+        in_specs=[VM, VM, VM, VM, AN],
         out_specs=[VM] * 3,
-        scratch_shapes=[pltpu.VMEM((nb + 1, KF, BLK), bf16), pltpu.VMEM((nb + 1, 8, BLK), f32)],
+        scratch_shapes=[
+            pltpu.VMEM((nb + 1, KF, BLK), bf16),
+            pltpu.VMEM((nb + 1, 8, BLK), f32),
+            pltpu.SMEM(lst.shape, i32),
+            pltpu.SemaphoreType.DMA(()),
+        ],
         compiler_params=pltpu.CompilerParams(vmem_limit_bytes=16 << 20),
         cost_estimate=pl.CostEstimate(flops=12 * nb * NP * BLK * BLK, bytes_accessed=8 << 20, transcendentals=nb * NP * BLK * BLK),
         name="density",
-    )(own, lo, hi, a_own, lst, total)
-
-
-def force_kernel(own, lo, hi, a_ref, town, tlo, thi, lst, total, out, b_ref, v_ref, acc):
+    )(own, lo, hi, a_own, lst)
+
+
+def force_kernel(own, lo, hi, a_ref, town, tlo, thi, listed, out, b_ref, v_ref, acc, lst, sem):
     nb = town.shape[0]
     hb = nb // 2
+    fetch = pltpu.make_async_copy(listed, lst, sem)
+    fetch.start()
 
     def sources(src, t, at, count):
         def body(i, _):
@@ -368,7 +377,8 @@
                 acc[code >> 8] += jnp.dot(v_ref[code & 255], weights.pop(g), preferred_element_type=f32)
         return 0
 
-    lax.fori_loop(0, total[0], main, 0)
+    fetch.wait()
+    lax.fori_loop(0, lst[lst.shape[0] - 1], main, 0)
 
     def finish(i, _):
         a = acc[i]
@@ -382,22 +392,24 @@
     lax.fori_loop(0, nb, finish, 0, unroll=8)
 
 
-def force(own, lo, hi, a, town, tlo, thi, lst, total):
+def force(own, lo, hi, a, town, tlo, thi, lst):
     nb = town.shape[0]
     return pl.pallas_call(
         force_kernel,
         out_shape=jax.ShapeDtypeStruct((3, nb * BLK), f32),
-        in_specs=[VM] * 7 + [SM, SM],
+        in_specs=[VM] * 7 + [AN],
         out_specs=VM,
         scratch_shapes=[
             pltpu.VMEM((nb + 1, KF, 2 * BLK), bf16),
             pltpu.VMEM((2 * nb, 16, BLK), bf16),
             pltpu.VMEM((nb + 1, 16, BLK), f32),
+            pltpu.SMEM(lst.shape, i32),
+            pltpu.SemaphoreType.DMA(()),
         ],
         compiler_params=pltpu.CompilerParams(vmem_limit_bytes=16 << 20),
         cost_estimate=pl.CostEstimate(flops=24 * nb * NP * BLK * BLK, bytes_accessed=8 << 20, transcendentals=2 * nb * NP * BLK * BLK),
         name="force",
-    )(own, lo, hi, a, town, tlo, thi, lst, total)
+    )(own, lo, hi, a, town, tlo, thi, lst)
 
 
 def on_device(positions, mass, smooth, cell_y, cell_z, cic_frac, pair_blocks, pair_count):
@@ -407,18 +419,18 @@
     up = [(i, (i + 1) % slabs) for i in range(slabs)]
     down = [((i + 1) % slabs, i) for i in range(slabs)]
     right = [(i, (i + 1) % cols) for i in range(cols)]
-    own, tail, head, pairs, counts = pack(
+    own, tail, head, lst = pack(
         positions, mass, smooth, cell_y, cell_z, cic_frac, pair_blocks.T, pair_count
     )
     lo = lax.ppermute(tail, "slab", up)
     hi = lax.ppermute(head, "slab", down)
-    grid, rim, a_own, lst, total = deposit_own(own, pairs, counts)
-    den, term, a = density(own, lo, hi, a_own, lst, total)
+    grid, rim, a_own = deposit_own(own)
+    den, term, a = density(own, lo, hi, a_own, lst)
     tlo = lax.ppermute(term[hb:], "slab", up)
     thi = lax.ppermute(term[:hb], "slab", down)
     grid, rim, edge_row = deposit_in(lo, grid, rim, term)
     rows = lax.ppermute(rim[:XP], "col", right)
-    acceleration = force(own, lo, hi, a, term, tlo, thi, lst, total)
+    acceleration = force(own, lo, hi, a, term, tlo, thi, lst)
     rows, acceleration = lax.optimization_barrier((rows, acceleration))
     grid = lax.dynamic_update_slice(grid, edge_row + rows[:, None], (0, 0, 0))
     return den.reshape(-1), acceleration, grid

time: 72.1 us -> 67.6 us (0.938)
  the two profiles are of different devices: /device:TPU:2 before, /device:TPU:8 now
where the time goes in v3:
time: 67.6 us; the launch traced here: 67.3 us
  Pallas kernels  36 us (53%)
  starting transfers between devices  26.6 us (39%)
  local copies, waits for them, and re-layouts  2.56 us (4%)
  waiting for transfers between devices  1.34 us (2%)
  between operations  0.77 us (1%)
    ppermute x1, starting transfers between devices, on_device(): hi = lax.ppermute(head, 'slab', down)  13.3 us
    pallas_call x1, Pallas kernels, force(): pl.pallas_call(force_kernel, out_shape=jax.ShapeDtypeStruct((3, nb * BLK)...  13.3 us
    pallas_call x1, Pallas kernels, density(): pl.pallas_call(density_kernel, out_shape=[jax.ShapeDtypeStruct((nb, BLK),...  8.48 us
    pallas_call x1, Pallas kernels, deposit_own(): pl.pallas_call(deposit_own_kernel, out_shape=[jax.ShapeDtypeStruct((XP, M...  7.19 us
    ppermute x1, starting transfers between devices, on_device(): thi = lax.ppermute(term[:hb], 'slab', down)  5.94 us
    pallas_call x1, Pallas kernels, deposit_in(): pl.pallas_call(deposit_in_kernel, out_shape=[jax.ShapeDtypeStruct((XP, MY...  4.43 us
    ppermute x1, starting transfers between devices, on_device(): rows = lax.ppermute(rim[:XP], 'col', right)  3.47 us
    pallas_call x1, Pallas kernels, pack(): pl.pallas_call(pack_kernel, out_shape=[jax.ShapeDtypeStruct((10, n), f32)...  2.69 us
  transfers between devices with their start and end apart: 5, of which 1 were waited for; matrix products, arithmetic and copies ran while one was open for 0% of the time, Pallas kernels for 37%

profile of v3, /device:TPU:8, one launch (start us, length us, event | category | flops | bytes accessed | tf_op | source)
XLA Modules:
  0.0 67.3 jit_solution(3571595184821763458)
XLA Ops:
  0.6 2.7 %pack.1 = (f32[10,8192]{1,0:T(8,128)}, f32[10,4096]{1,0:T(8,128)}, f32[5,4096]{1,0:T(8,128)}, s32[649]{0:T(1024)}) custom-call(f32[3,8192]{1,0:T(4,128)} %pos.1, f32[1,8192]{1,0:T(1,128)} %bitcast.7, f32[1,8192]{1,0:T(1,128)} %bitcast.8, s32[1,8192]{1,0:T(1,128)} %bitcast.9, s32[1,8192]{1,0:T(1,128)} %bitcast.10, f32[3,8192]{1,0:T(4,128)} %frac.1, ...), custom_call_target="tpu_custom_call" | custom-call | tf_op jit(solution)/shard_map/pack/pallas_call | solution.py:76
  3.3 13.3 %collective-permute-start.1 = (f32[5,4096]{1,0:T(8,128)}, f32[5,4096]{1,0:T(8,128)S(1)}, u32[]{:S(2)}, u32[]{:S(2)}) collective-permute-start(f32[5,4096]{1,0:T(8,128)} %get-tuple-element.20), channel_id=1, source_target_pairs={{8,0},{16,8},{24,16},{32,24},{40,32},{48,40},{56,48},{64,56},{72,6... | collective-permute-start | bytes 245768 | tf_op jit(solution)/shard_map/ppermute | solution.py:426
  16.6 1.9 %collective-permute-start = (f32[10,4096]{1,0:T(8,128)}, f32[10,4096]{1,0:T(8,128)S(1)}, u32[]{:S(2)}, u32[]{:S(2)}) collective-permute-start(f32[10,4096]{1,0:T(8,128)} %get-tuple-element.19), channel_id=1, source_target_pairs={{0,8},{8,16},{16,24},{24,32},{32,40},{40,48},{48,56},{56,64},{64,7... | collective-permute-start | bytes 491528 | tf_op jit(solution)/shard_map/ppermute | solution.py:425
  18.6 0.0 copy-start
  18.6 1.0 %copy-done = f32[10,8192]{1,0:T(8,128)S(1)} copy-done((f32[10,8192]{1,0:T(8,128)S(1)}, f32[10,8192]{1,0:T(8,128)}, u32[]{:S(2)}) %copy-start) | copy-done | bytes 327704
  19.6 0.0 copy-start.2
  19.6 7.2 %deposit_own.1 = (f32[2,128,1024]{2,1,0:T(8,128)S(1)}, f32[8,1024]{1,0:T(8,128)S(1)}, bf16[64,128,48]{2,1,0:T(8,128)(2,1)S(1)}) custom-call(f32[10,8192]{1,0:T(8,128)S(1)} %copy-done), custom_call_target="tpu_custom_call" | custom-call | flops 4294967296 | bytes 4194304 | tf_op jit(solution)/shard_map/deposit_own/pallas_call | solution.py:215
  26.8 0.0 collective-permute-done.1.hi
  26.8 1.3 %collective-permute-done.lo.st = f32[10,4096]{1,0:T(8,128)S(1)} collective-permute-done((f32[10,4096]{1,0:T(8,128)}, f32[10,4096]{1,0:T(8,128)S(1)}, u32[]{:S(2)}, u32[]{:S(2)}) %collective-permute-start) | collective-permute-done | bytes 163872 | tf_op jit(solution)/shard_map/ppermute | solution.py:425
  28.2 0.0 copy-done.2
  28.2 0.0 copy-start.1
  28.2 8.5 %density.1 = (f32[64,128]{1,0:T(8,128)}, f32[64,128]{1,0:T(8,128)S(1)}, bf16[128,128,48]{2,1,0:T(8,128)(2,1)S(1)}) custom-call(f32[10,8192]{1,0:T(8,128)S(1)} %copy-done, f32[10,4096]{1,0:T(8,128)S(1)} %collective-permute-done.lo.st, f32[5,4096]{1,0:T(8,128)S(1)} %collective-permute-done.1.hi, bf16[64,128,48]{2,1,0:T(8,128)(2,1)S(1)} %get-tuple-element.21.a_own, ...), custom_call_target="tpu_custom_call" | custom-call | flops 113246208 | bytes 8388608 | tf_op jit(solution)/shard_map/density/pallas_call | solution.py:302
  36.7 5.9 %collective-permute-start.4 = (f32[32,128]{1,0:T(8,128)S(1)}, f32[32,128]{1,0:T(8,128)S(1)}, u32[]{:S(2)}, u32[]{:S(2)}) collective-permute-start(f32[32,128]{1,0:T(8,128)S(1)} %get-tuple-element.33), channel_id=1, source_target_pairs={{8,0},{16,8},{24,16},{32,24},{40,32},{48,40},{56,48},{64,56},{72,6... | collective-permute-start | bytes 49160 | tf_op jit(solution)/shard_map/ppermute | solution.py:430
  42.6 1.9 %collective-permute-start.3 = (f32[32,128]{1,0:T(8,128)S(1)}, f32[32,128]{1,0:T(8,128)S(1)}, u32[]{:S(2)}, u32[]{:S(2)}) collective-permute-start(f32[32,128]{1,0:T(8,128)S(1)} %get-tuple-element.34), channel_id=1, source_target_pairs={{0,8},{8,16},{16,24},{24,32},{32,40},{40,48},{48,56},{56,64},{64,7... | collective-permute-start | bytes 49160 | tf_op jit(solution)/shard_map/ppermute | solution.py:429
  44.5 4.4 %deposit_in.1 = (f32[2,128,1024]{2,1,0:T(8,128)}, f32[8,1024]{1,0:T(8,128)S(1)}, f32[2,1,1024]{2,1,0:T(1,128)S(1)}) custom-call(f32[10,4096]{1,0:T(8,128)S(1)} %collective-permute-done.lo.st, f32[2,128,1024]{2,1,0:T(8,128)S(1)} %get-tuple-element.24.g_in, f32[8,1024]{1,0:T(8,128)S(1)} %get-tuple-element.25.r_in, f32[64,128]{1,0:T(8,128)S(1)} %get-tuple-element.26.after.town), custom_call_target="tpu_custom_call" | custom-call | flops 1073741824 | bytes 4194304 | tf_op jit(solution)/shard_map/deposit_in/pallas_call | solution.py:248
  49.0 3.5 %collective-permute-start.2 = (f32[2,1024]{1,0:T(2,128)S(1)}, f32[2,1024]{1,0:T(2,128)S(1)}, u32[]{:S(2)}, u32[]{:S(2)}) collective-permute-start(f32[2,1024]{1,0:T(2,128)S(1)} %slice.9), channel_id=1, source_target_pairs={{0,1},{1,2},{2,3},{3,4},{4,5},{5,6},{6,7},{7,0},{8,9},{9,10},{10,1... | collective-permute-start | bytes 24584 | tf_op jit(solution)/shard_map/ppermute | solution.py:432
  52.4 0.0 collective-permute-done.4.thi
  52.4 0.0 collective-permute-done.3.tlo
  52.5 0.0 copy-done.1
  52.5 13.3 %force.1 = f32[3,8192]{1,0:T(4,128)} custom-call(f32[10,8192]{1,0:T(8,128)S(1)} %copy-done.1, f32[10,4096]{1,0:T(8,128)S(1)} %collective-permute-done.lo.st, f32[5,4096]{1,0:T(8,128)S(1)} %collective-permute-done.1.hi, bf16[128,128,48]{2,1,0:T(8,128)(2,1)S(1)} %get-tuple-element.28.a_ref, f32[64,128]{1,0:T(8,128)S(1)} %get-tuple-element.26.after.town, ...), custom_call_target="tpu_custom_call" | custom-call | flops 226492416 | bytes 8388608 | tf_op jit(solution)/shard_map/force/pallas_call | solution.py:397
  65.7 0.0 collective-permute-done.2
  65.8 1.5 %dynamic_update_slice.3 = f32[2,128,1024]{2,1,0:T(8,128)} dynamic-update-slice(f32[2,128,1024]{2,1,0:T(8,128)} %get-tuple-element.30, f32[2,1,1024]{2,1,0:T(1,128)S(1)} %reshape_add_fusion, s32[]{:T(128)} %constant.0.clone.1, s32[]{:T(128)} %constant.0.clone.1, s32[]{:T(128)} %constant.0.clone.1) | dynamic-update-slice | bytes 16388 | tf_op jit(solution)/shard_map/dynamic_update_slice | solution.py:435
  (3 shorter events, 0.0 us)
Async XLA Ops:
  3.3 23.5 %collective-permute-start.1 = (f32[5,4096]{1,0:T(8,128)}, f32[5,4096]{1,0:T(8,128)S(1)}, u32[]{:S(2)}, u32[]{:S(2)}) collective-permute-start(f32[5,4096]{1,0:T(8,128)} %get-tuple-element.20), channel_id=1, source_target_pairs={{8,0},{16,8},{24,16},{32,24},{40,32},{48,40},{56,48},{64,56},{72,6... | collective-permute-start | bytes 245768 | tf_op jit(solution)/shard_map/ppermute | solution.py:426
  16.6 11.5 %collective-permute-start = (f32[10,4096]{1,0:T(8,128)}, f32[10,4096]{1,0:T(8,128)S(1)}, u32[]{:S(2)}, u32[]{:S(2)}) collective-permute-start(f32[10,4096]{1,0:T(8,128)} %get-tuple-element.19), channel_id=1, source_target_pairs={{0,8},{8,16},{16,24},{24,32},{32,40},{40,48},{48,56},{56,64},{64,7... | collective-permute-start | bytes 491528 | tf_op jit(solution)/shard_map/ppermute | solution.py:425
  18.6 1.0 %copy-start = (f32[10,8192]{1,0:T(8,128)S(1)}, f32[10,8192]{1,0:T(8,128)}, u32[]{:S(2)}) copy-start(f32[10,8192]{1,0:T(8,128)} %get-tuple-element.18.st.own) | copy-start | bytes 983044
  19.6 8.5 %copy-start.2 = (s32[649]{0:T(1024)S(1)}, s32[649]{0:T(1024)}, u32[]{:S(2)}) copy-start(s32[649]{0:T(1024)} %get-tuple-element.22.listed) | copy-start | bytes 7792
  28.2 24.3 %copy-start.1 = (f32[10,8192]{1,0:T(8,128)S(1)}, f32[10,8192]{1,0:T(8,128)}, u32[]{:S(2)}) copy-start(f32[10,8192]{1,0:T(8,128)} %get-tuple-element.18.st.own) | copy-start | bytes 983044
  36.7 15.8 %collective-permute-start.4 = (f32[32,128]{1,0:T(8,128)S(1)}, f32[32,128]{1,0:T(8,128)S(1)}, u32[]{:S(2)}, u32[]{:S(2)}) collective-permute-start(f32[32,128]{1,0:T(8,128)S(1)} %get-tuple-element.33), channel_id=1, source_target_pairs={{8,0},{16,8},{24,16},{32,24},{40,32},{48,40},{56,48},{64,56},{72,6... | collective-permute-start | bytes 49160 | tf_op jit(solution)/shard_map/ppermute | solution.py:430
  42.6 9.9 %collective-permute-start.3 = (f32[32,128]{1,0:T(8,128)S(1)}, f32[32,128]{1,0:T(8,128)S(1)}, u32[]{:S(2)}, u32[]{:S(2)}) collective-permute-start(f32[32,128]{1,0:T(8,128)S(1)} %get-tuple-element.34), channel_id=1, source_target_pairs={{0,8},{8,16},{16,24},{24,32},{32,40},{40,48},{48,56},{56,64},{64,7... | collective-permute-start | bytes 49160 | tf_op jit(solution)/shard_map/ppermute | solution.py:429
  49.0 16.8 %collective-permute-start.2 = (f32[2,1024]{1,0:T(2,128)S(1)}, f32[2,1024]{1,0:T(2,128)S(1)}, u32[]{:S(2)}, u32[]{:S(2)}) collective-permute-start(f32[2,1024]{1,0:T(2,128)S(1)} %slice.9), channel_id=1, source_target_pairs={{0,1},{1,2},{2,3},{3,4},{4,5},{5,6},{6,7},{7,0},{8,9},{9,10},{10,1... | collective-permute-start | bytes 24584 | tf_op jit(solution)/shard_map/ppermute | solution.py:432

commit v4 on v3

--- a/solution.py
+++ b/solution.py
@@ -14,9 +14,10 @@
 MZ = 1024
 LOG2E = 1.4426950408889634
 KF = 48
-GROUP = 32
+GROUP = 64
+REST = 16
 SPAN = 1024
-ZB = 512
+ZB = 1024
 
 f32 = jnp.float32
 bf16 = jnp.bfloat16
@@ -57,9 +58,9 @@
         for k in range(NP):
             lst[at + k] = spairs[k, b] + b * 256
         at = at + scounts[0, b]
-    for k in range(GROUP):
+    for k in range(REST):
         lst[at + k] = i32(nb * 256)
-    lst[lst.shape[0] - 1] = (at + GROUP - 1) // GROUP
+    lst[lst.shape[0] - 1] = at
     own[0:3] = vpos[...]
     own[3:4] = vmass[...]
     own[4:5] = vsmooth[...]
@@ -79,7 +80,7 @@
             jax.ShapeDtypeStruct((10, n), f32),
             jax.ShapeDtypeStruct((10, n // 2), f32),
             jax.ShapeDtypeStruct((5, n // 2), f32),
-            jax.ShapeDtypeStruct((nb * NP + NP + 2 * GROUP,), i32),
+            jax.ShapeDtypeStruct((nb * NP + NP + 2 * REST,), i32),
         ],
         in_specs=[HB] * 8,
         out_specs=[VM] * 3 + [SM],
@@ -190,6 +191,13 @@
     return lax.dot_general(rows_ref[...], hat_table(top, hit_ref[...], tiles), NT, preferred_element_type=f32)
 
 
+def deposit_dot_one(z, rows_ref, top_ref, hit_ref):
+    tiles = ZB // 16
+    top = (top_ref[...] - (z * tiles).astype(f32)).astype(bf16)
+    u = lax.dot_general(hat_table(top, hit_ref[...], tiles), rows_ref[...], NT, preferred_element_type=f32)
+    return u.T
+
+
 def deposit_own_kernel(st, grid, rim, a_own, rows1, top1, hit1, rows2, top2, hit2):
     n = st.shape[1]
     half = n // 2
@@ -201,7 +209,7 @@
     def body(z, _):
         at = lanes(z, ZB)
         u = deposit_dot(z, rows1, top1, hit1)
-        v = deposit_dot(z, rows2, top2, hit2)
+        v = deposit_dot_one(z, rows2, top2, hit2)
         grid[0, :, at] = u[0:MYD]
         grid[1, :, at] = u[MYD : 2 * MYD] + v[0:MYD]
         rim[:, at] = u[2 * MYD : 2 * MYD + 8] + v[MYD : MYD + 8]
@@ -234,7 +242,7 @@
 
     def body(z, _):
         at = lanes(z, ZB)
-        u = deposit_dot(z, rows, top, hit)
+        u = deposit_dot_one(z, rows, top, hit)
         grid[0, :, at] = g_in[0, :, at] + u[0:MYD]
         grid[1, :, at] = g_in[1, :, at]
         rim[:, at] = r_in[:, at] + u[MYD : MYD + 8]
@@ -259,6 +267,22 @@
         cost_estimate=pl.CostEstimate(flops=2 * st.shape[1] * MYD * MZ, bytes_accessed=4 << 20, transcendentals=0),
         name="deposit_in",
     )(st, g, r, after)
+
+
+def for_groups(lst, work):
+    live = lst[lst.shape[0] - 1]
+    full = live // GROUP
+
+    def whole(it, _):
+        work(it * GROUP, GROUP)
+        return 0
+
+    def rest(it, _):
+        work(full * GROUP + it * REST, REST)
+        return 0
+
+    lax.fori_loop(0, full, whole, 0)
+    lax.fori_loop(0, (live - full * GROUP + REST - 1) // REST, rest, 0)
 
 
 def density_kernel(own, lo, hi, a_own, listed, den, term, a_ref, b_ref, acc, lst, sem):
@@ -283,15 +307,14 @@
     b_ref[nb] = jnp.zeros((KF, BLK), bf16)
     acc[...] = jnp.zeros_like(acc)
 
-    def main(it, _):
-        for g in range(GROUP):
-            code = lst[it * GROUP + g]
+    def work(at, size):
+        for g in range(size):
+            code = lst[at + g]
             e = jnp.dot(a_ref[code & 255], b_ref[code >> 8], preferred_element_type=f32)
             acc[code >> 8] += jnp.exp2(e).reshape(BLK // 8, 8, BLK).sum(0)
-        return 0
 
     fetch.wait()
-    lax.fori_loop(0, lst[lst.shape[0] - 1], main, 0)
+    for_groups(lst, work)
     d = acc[0:nb].sum(1) * (1.0 / (NP * BLK))
     den[...] = d
     term[...] = jnp.exp2(jnp.log2(d) * (-1.0 / 3.0))
@@ -356,29 +379,27 @@
     lax.fori_loop(0, nb, own_tile, 0, unroll=4)
     b_ref[nb] = jnp.ones((KF, 2 * BLK), bf16)
     acc[...] = jnp.zeros_like(acc)
-    lag = 8
-
-    def main(it, _):
-        codes = [lst[it * GROUP + g] for g in range(GROUP)]
+    def work(at, size):
+        lag = min(8, size // 4)
+        codes = [lst[at + g] for g in range(size)]
         forms = {}
         weights = {}
-        for step in range(GROUP + 2 * lag):
-            if step < GROUP:
+        for step in range(size + 2 * lag):
+            if step < size:
                 code = codes[step]
                 forms[step] = jnp.dot(a_ref[code & 255], b_ref[code >> 8], preferred_element_type=f32)
             g = step - lag
-            if 0 <= g < GROUP:
+            if 0 <= g < size:
                 e = forms.pop(g)
                 r = pl.reciprocal(e[:, BLK : 2 * BLK], approx=True)
                 weights[g] = (jnp.exp2(e[:, 0:BLK] * r) * r).astype(bf16)
             g = step - 2 * lag
-            if 0 <= g < GROUP:
+            if 0 <= g < size:
                 code = codes[g]
                 acc[code >> 8] += jnp.dot(v_ref[code & 255], weights.pop(g), preferred_element_type=f32)
-        return 0
 
     fetch.wait()
-    lax.fori_loop(0, lst[lst.shape[0] - 1], main, 0)
+    for_groups(lst, work)
 
     def finish(i, _):
         a = acc[i]

time: 67.6 us -> 63.1 us (0.933)
  the two profiles are of different devices: /device:TPU:8 before, /device:TPU:16 now
where the time goes in v4:
time: 63.1 us; the launch traced here: 62.7 us
  Pallas kernels  31.7 us (50%)
  starting transfers between devices  24.4 us (39%)
  waiting for transfers between devices  3.37 us (5%)
  local copies, waits for them, and re-layouts  2.56 us (4%)
  between operations  0.75 us (1%)
    ppermute x1, starting transfers between devices, on_device(): hi = lax.ppermute(head, 'slab', down)  13.3 us
    pallas_call x1, Pallas kernels, force(): pl.pallas_call(force_kernel, out_shape=jax.ShapeDtypeStruct((3, nb * BLK)...  12.3 us
    pallas_call x1, Pallas kernels, density(): pl.pallas_call(density_kernel, out_shape=[jax.ShapeDtypeStruct((nb, BLK),...  7.72 us
    pallas_call x1, Pallas kernels, deposit_own(): pl.pallas_call(deposit_own_kernel, out_shape=[jax.ShapeDtypeStruct((XP, M...  5.61 us
    ppermute x1, starting transfers between devices, on_device(): thi = lax.ppermute(term[:hb], 'slab', down)  4.37 us
    pallas_call x1, Pallas kernels, deposit_in(): pl.pallas_call(deposit_in_kernel, out_shape=[jax.ShapeDtypeStruct((XP, MY...  3.41 us
    ppermute x1, waiting for transfers between devices, on_device(): lo = lax.ppermute(tail, 'slab', up)  2.92 us
    ppermute x1, starting transfers between devices, on_device(): rows = lax.ppermute(rim[:XP], 'col', right)  2.87 us
  transfers between devices with their start and end apart: 5, of which 2 were waited for; matrix products, arithmetic and copies ran while one was open for 0% of the time, Pallas kernels for 34%

profile of v4, /device:TPU:16, one launch (start us, length us, event | category | flops | bytes accessed | tf_op | source)
XLA Modules:
  0.0 62.7 jit_solution(12525281156499624659)
XLA Ops:
  0.6 2.7 %pack.1 = (f32[10,8192]{1,0:T(8,128)}, f32[10,4096]{1,0:T(8,128)}, f32[5,4096]{1,0:T(8,128)}, s32[617]{0:T(1024)}) custom-call(f32[3,8192]{1,0:T(4,128)} %pos.1, f32[1,8192]{1,0:T(1,128)} %bitcast.7, f32[1,8192]{1,0:T(1,128)} %bitcast.8, s32[1,8192]{1,0:T(1,128)} %bitcast.9, s32[1,8192]{1,0:T(1,128)} %bitcast.10, f32[3,8192]{1,0:T(4,128)} %frac.1, ...), custom_call_target="tpu_custom_call" | custom-call | tf_op jit(solution)/shard_map/pack/pallas_call | solution.py:77
  3.3 13.3 %collective-permute-start.1 = (f32[5,4096]{1,0:T(8,128)}, f32[5,4096]{1,0:T(8,128)S(1)}, u32[]{:S(2)}, u32[]{:S(2)}) collective-permute-start(f32[5,4096]{1,0:T(8,128)} %get-tuple-element.20), channel_id=1, source_target_pairs={{8,0},{16,8},{24,16},{32,24},{40,32},{48,40},{56,48},{64,56},{72,6... | collective-permute-start | bytes 245768 | tf_op jit(solution)/shard_map/ppermute | solution.py:447
  16.6 1.9 %collective-permute-start = (f32[10,4096]{1,0:T(8,128)}, f32[10,4096]{1,0:T(8,128)S(1)}, u32[]{:S(2)}, u32[]{:S(2)}) collective-permute-start(f32[10,4096]{1,0:T(8,128)} %get-tuple-element.19), channel_id=1, source_target_pairs={{0,8},{8,16},{16,24},{24,32},{32,40},{40,48},{48,56},{56,64},{64,7... | collective-permute-start | bytes 491528 | tf_op jit(solution)/shard_map/ppermute | solution.py:446
  18.6 0.0 copy-start
  18.6 1.0 %copy-done = f32[10,8192]{1,0:T(8,128)S(1)} copy-done((f32[10,8192]{1,0:T(8,128)S(1)}, f32[10,8192]{1,0:T(8,128)}, u32[]{:S(2)}) %copy-start) | copy-done | bytes 327704
  19.6 0.0 copy-start.2
  19.6 5.6 %deposit_own.1 = (f32[2,128,1024]{2,1,0:T(8,128)S(1)}, f32[8,1024]{1,0:T(8,128)S(1)}, bf16[64,128,48]{2,1,0:T(8,128)(2,1)S(1)}) custom-call(f32[10,8192]{1,0:T(8,128)S(1)} %copy-done), custom_call_target="tpu_custom_call" | custom-call | flops 4294967296 | bytes 4194304 | tf_op jit(solution)/shard_map/deposit_own/pallas_call | solution.py:223
  25.2 0.0 collective-permute-done.1.hi
  25.2 2.9 %collective-permute-done.lo.st = f32[10,4096]{1,0:T(8,128)S(1)} collective-permute-done((f32[10,4096]{1,0:T(8,128)}, f32[10,4096]{1,0:T(8,128)S(1)}, u32[]{:S(2)}, u32[]{:S(2)}) %collective-permute-start) | collective-permute-done | bytes 163872 | tf_op jit(solution)/shard_map/ppermute | solution.py:446
  28.1 0.0 copy-done.2
  28.1 0.0 copy-start.1
  28.1 7.7 %density.1 = (f32[64,128]{1,0:T(8,128)}, f32[64,128]{1,0:T(8,128)S(1)}, bf16[128,128,48]{2,1,0:T(8,128)(2,1)S(1)}) custom-call(f32[10,8192]{1,0:T(8,128)S(1)} %copy-done, f32[10,4096]{1,0:T(8,128)S(1)} %collective-permute-done.lo.st, f32[5,4096]{1,0:T(8,128)S(1)} %collective-permute-done.1.hi, bf16[64,128,48]{2,1,0:T(8,128)(2,1)S(1)} %get-tuple-element.21.a_own, ...), custom_call_target="tpu_custom_call" | custom-call | flops 113246208 | bytes 8388608 | tf_op jit(solution)/shard_map/density/pallas_call | solution.py:325
  35.9 4.4 %collective-permute-start.4 = (f32[32,128]{1,0:T(8,128)S(1)}, f32[32,128]{1,0:T(8,128)S(1)}, u32[]{:S(2)}, u32[]{:S(2)}) collective-permute-start(f32[32,128]{1,0:T(8,128)S(1)} %get-tuple-element.33), channel_id=1, source_target_pairs={{8,0},{16,8},{24,16},{32,24},{40,32},{48,40},{56,48},{64,56},{72,6... | collective-permute-start | bytes 49160 | tf_op jit(solution)/shard_map/ppermute | solution.py:451
  40.3 1.9 %collective-permute-start.3 = (f32[32,128]{1,0:T(8,128)S(1)}, f32[32,128]{1,0:T(8,128)S(1)}, u32[]{:S(2)}, u32[]{:S(2)}) collective-permute-start(f32[32,128]{1,0:T(8,128)S(1)} %get-tuple-element.34), channel_id=1, source_target_pairs={{0,8},{8,16},{16,24},{24,32},{32,40},{40,48},{48,56},{56,64},{64,7... | collective-permute-start | bytes 49160 | tf_op jit(solution)/shard_map/ppermute | solution.py:450
  42.2 3.4 %deposit_in.1 = (f32[2,128,1024]{2,1,0:T(8,128)}, f32[8,1024]{1,0:T(8,128)S(1)}, f32[2,1,1024]{2,1,0:T(1,128)S(1)}) custom-call(f32[10,4096]{1,0:T(8,128)S(1)} %collective-permute-done.lo.st, f32[2,128,1024]{2,1,0:T(8,128)S(1)} %get-tuple-element.24.g_in, f32[8,1024]{1,0:T(8,128)S(1)} %get-tuple-element.25.r_in, f32[64,128]{1,0:T(8,128)S(1)} %get-tuple-element.26.after.town), custom_call_target="tpu_custom_call" | custom-call | flops 1073741824 | bytes 4194304 | tf_op jit(solution)/shard_map/deposit_in/pallas_call | solution.py:256
  45.6 2.9 %collective-permute-start.2 = (f32[2,1024]{1,0:T(2,128)S(1)}, f32[2,1024]{1,0:T(2,128)S(1)}, u32[]{:S(2)}, u32[]{:S(2)}) collective-permute-start(f32[2,1024]{1,0:T(2,128)S(1)} %slice.9), channel_id=1, source_target_pairs={{0,1},{1,2},{2,3},{3,4},{4,5},{5,6},{6,7},{7,0},{8,9},{9,10},{10,1... | collective-permute-start | bytes 24584 | tf_op jit(solution)/shard_map/ppermute | solution.py:453
  48.5 0.0 collective-permute-done.4.thi
  48.5 0.4 collective-permute-done.3.tlo
  48.9 0.0 copy-done.1
  48.9 12.3 %force.1 = f32[3,8192]{1,0:T(4,128)} custom-call(f32[10,8192]{1,0:T(8,128)S(1)} %copy-done.1, f32[10,4096]{1,0:T(8,128)S(1)} %collective-permute-done.lo.st, f32[5,4096]{1,0:T(8,128)S(1)} %collective-permute-done.1.hi, bf16[128,128,48]{2,1,0:T(8,128)(2,1)S(1)} %get-tuple-element.28.a_ref, f32[64,128]{1,0:T(8,128)S(1)} %get-tuple-element.26.after.town, ...), custom_call_target="tpu_custom_call" | custom-call | flops 226492416 | bytes 8388608 | tf_op jit(solution)/shard_map/force/pallas_call | solution.py:418
  61.2 0.0 collective-permute-done.2
  61.2 1.5 %dynamic_update_slice.3 = f32[2,128,1024]{2,1,0:T(8,128)} dynamic-update-slice(f32[2,128,1024]{2,1,0:T(8,128)} %get-tuple-element.30, f32[2,1,1024]{2,1,0:T(1,128)S(1)} %reshape_add_fusion, s32[]{:T(128)} %constant.0.clone.1, s32[]{:T(128)} %constant.0.clone.1, s32[]{:T(128)} %constant.0.clone.1) | dynamic-update-slice | bytes 16388 | tf_op jit(solution)/shard_map/dynamic_update_slice | solution.py:456
  (3 shorter events, 0.0 us)
Async XLA Ops:
  3.3 21.9 %collective-permute-start.1 = (f32[5,4096]{1,0:T(8,128)}, f32[5,4096]{1,0:T(8,128)S(1)}, u32[]{:S(2)}, u32[]{:S(2)}) collective-permute-start(f32[5,4096]{1,0:T(8,128)} %get-tuple-element.20), channel_id=1, source_target_pairs={{8,0},{16,8},{24,16},{32,24},{40,32},{48,40},{56,48},{64,56},{72,6... | collective-permute-start | bytes 245768 | tf_op jit(solution)/shard_map/ppermute | solution.py:447
  16.6 11.5 %collective-permute-start = (f32[10,4096]{1,0:T(8,128)}, f32[10,4096]{1,0:T(8,128)S(1)}, u32[]{:S(2)}, u32[]{:S(2)}) collective-permute-start(f32[10,4096]{1,0:T(8,128)} %get-tuple-element.19), channel_id=1, source_target_pairs={{0,8},{8,16},{16,24},{24,32},{32,40},{40,48},{48,56},{56,64},{64,7... | collective-permute-start | bytes 491528 | tf_op jit(solution)/shard_map/ppermute | solution.py:446
  18.6 1.0 %copy-start = (f32[10,8192]{1,0:T(8,128)S(1)}, f32[10,8192]{1,0:T(8,128)}, u32[]{:S(2)}) copy-start(f32[10,8192]{1,0:T(8,128)} %get-tuple-element.18.st.own) | copy-start | bytes 983044
  19.6 8.5 %copy-start.2 = (s32[617]{0:T(1024)S(1)}, s32[617]{0:T(1024)}, u32[]{:S(2)}) copy-start(s32[617]{0:T(1024)} %get-tuple-element.22.listed) | copy-start | bytes 7408
  28.1 20.8 %copy-start.1 = (f32[10,8192]{1,0:T(8,128)S(1)}, f32[10,8192]{1,0:T(8,128)}, u32[]{:S(2)}) copy-start(f32[10,8192]{1,0:T(8,128)} %get-tuple-element.18.st.own) | copy-start | bytes 983044
  35.9 12.6 %collective-permute-start.4 = (f32[32,128]{1,0:T(8,128)S(1)}, f32[32,128]{1,0:T(8,128)S(1)}, u32[]{:S(2)}, u32[]{:S(2)}) collective-permute-start(f32[32,128]{1,0:T(8,128)S(1)} %get-tuple-element.33), channel_id=1, source_target_pairs={{8,0},{16,8},{24,16},{32,24},{40,32},{48,40},{56,48},{64,56},{72,6... | collective-permute-start | bytes 49160 | tf_op jit(solution)/shard_map/ppermute | solution.py:451
  40.3 8.7 %collective-permute-start.3 = (f32[32,128]{1,0:T(8,128)S(1)}, f32[32,128]{1,0:T(8,128)S(1)}, u32[]{:S(2)}, u32[]{:S(2)}) collective-permute-start(f32[32,128]{1,0:T(8,128)S(1)} %get-tuple-element.34), channel_id=1, source_target_pairs={{0,8},{8,16},{16,24},{24,32},{32,40},{40,48},{48,56},{56,64},{64,7... | collective-permute-start | bytes 49160 | tf_op jit(solution)/shard_map/ppermute | solution.py:450
  45.6 15.6 %collective-permute-start.2 = (f32[2,1024]{1,0:T(2,128)S(1)}, f32[2,1024]{1,0:T(2,128)S(1)}, u32[]{:S(2)}, u32[]{:S(2)}) collective-permute-start(f32[2,1024]{1,0:T(2,128)S(1)} %slice.9), channel_id=1, source_target_pairs={{0,1},{1,2},{2,3},{3,4},{4,5},{5,6},{6,7},{7,0},{8,9},{9,10},{10,1... | collective-permute-start | bytes 24584 | tf_op jit(solution)/shard_map/ppermute | solution.py:453

commit v5 on v4

--- a/solution.py
+++ b/solution.py
@@ -53,11 +53,15 @@
     for copy in copies[-2:] + copies[:-2]:
         copy.wait()
     nb = counts.shape[1]
-    at = i32(0)
+    hb = nb // 2
+    for b in range(hb):
+        for n, (row, partner) in enumerate(((b, hb + b), (b, nb + b), (hb + b, hb + b), (hb + b, nb + b))):
+            lst[4 * b + n] = i32(row * 256 + partner)
+    at = i32(2 * nb)
     for b in range(nb):
-        for k in range(NP):
-            lst[at + k] = spairs[k, b] + b * 256
-        at = at + scounts[0, b]
+        for n, k in enumerate((1 if b < hb else 2,) + tuple(range(3, NP))):
+            lst[at + n] = spairs[k, b] + b * 256
+        at = at + scounts[0, b] - 2
     for k in range(REST):
         lst[at + k] = i32(nb * 256)
     lst[lst.shape[0] - 1] = at
@@ -125,6 +129,18 @@
     one = jnp.ones_like(m)
     rows = jnp.concatenate([x, norm_sq(x), jnp.log2(m), 0.5 * s * s, one, jnp.zeros_like(one)], 0)
     return stack_a(rows).T
+
+
+def density_tile(st):
+    x, s = st[0:3], st[4:5]
+    one = jnp.ones_like(s)
+    zero = jnp.zeros_like(s)
+    c = LOG2E / (s * s)
+    return stack_b(jnp.concatenate([2.0 * c * x, -c, one, zero, -c * norm_sq(x), zero], 0))
+
+
+def column_sums(e):
+    return jnp.exp2(e).reshape(e.shape[0] // 8, 8, BLK).sum(0)
 
 
 def fill_partners(src, a_ref, at, count):
@@ -198,10 +214,23 @@
     return u.T
 
 
-def deposit_own_kernel(st, grid, rim, a_own, rows1, top1, hit1, rows2, top2, hit2):
+def deposit_own_kernel(st, grid, rim, a_own, start, rows1, top1, hit1, rows2, top2, hit2):
     n = st.shape[1]
     half = n // 2
-    fill_partners(st, a_own, 0, a_own.shape[0])
+    nb = a_own.shape[0]
+    hb = nb // 2
+    fill_partners(st, a_own, 0, nb)
+
+    def own_pairs(i, _):
+        for u in range(8):
+            b = i * 8 + u
+            w = jnp.concatenate([density_tile(st[0:5, lanes(b)]), density_tile(st[0:5, lanes(b + hb)])], 1)
+            e = jnp.dot(jnp.concatenate([a_own[b], a_own[b + hb]], 0), w, preferred_element_type=f32)
+            start[b] = column_sums(e[:, 0:BLK])
+            start[b + hb] = column_sums(e[:, BLK : 2 * BLK])
+        return 0
+
+    lax.fori_loop(0, hb // 8, own_pairs, 0)
     for k in range(half // SPAN):
         fill_tables(st, 0, k, (0, 1), (0, 1), rows1, top1, hit1)
         fill_tables(st, half, k, (0,), (1,), rows2, top2, hit2)
@@ -226,9 +255,10 @@
             jax.ShapeDtypeStruct((XP, MYD, MZ), f32),
             jax.ShapeDtypeStruct((8, MZ), f32),
             jax.ShapeDtypeStruct((nb, BLK, KF), bf16),
+            jax.ShapeDtypeStruct((nb, 8, BLK), f32),
         ],
         in_specs=[VM],
-        out_specs=[VM] * 3,
+        out_specs=[VM] * 4,
         scratch_shapes=table_scratch(2, st.shape[1] // 2) + table_scratch(1, st.shape[1] // 2),
         compiler_params=pltpu.CompilerParams(vmem_limit_bytes=16 << 20),
         cost_estimate=pl.CostEstimate(flops=4 * st.shape[1] * MYD * MZ, bytes_accessed=4 << 20, transcendentals=0),
@@ -269,23 +299,23 @@
     )(st, g, r, after)
 
 
-def for_groups(lst, work):
-    live = lst[lst.shape[0] - 1]
+def for_groups(lst, work, skip):
+    live = lst[lst.shape[0] - 1] - skip
     full = live // GROUP
 
     def whole(it, _):
-        work(it * GROUP, GROUP)
+        work(skip + it * GROUP, GROUP)
         return 0
 
     def rest(it, _):
-        work(full * GROUP + it * REST, REST)
+        work(skip + full * GROUP + it * REST, REST)
         return 0
 
     lax.fori_loop(0, full, whole, 0)
     lax.fori_loop(0, (live - full * GROUP + REST - 1) // REST, rest, 0)
 
 
-def density_kernel(own, lo, hi, a_own, listed, den, term, a_ref, b_ref, acc, lst, sem):
+def density_kernel(own, lo, hi, a_own, start, listed, den, term, a_ref, b_ref, acc, lst, sem):
     nb = den.shape[0]
     hb = nb // 2
     fetch = pltpu.make_async_copy(listed, lst, sem)
@@ -295,32 +325,28 @@
     a_ref[hb : hb + nb] = a_own[...]
 
     def own_tile(i, _):
-        st = own[0:5, lanes(i)]
-        x, s = st[0:3], st[4:5]
-        one = jnp.ones_like(s)
-        zero = jnp.zeros_like(s)
-        c = LOG2E / (s * s)
-        b_ref[i] = stack_b(jnp.concatenate([2.0 * c * x, -c, one, zero, -c * norm_sq(x), zero], 0))
+        b_ref[i] = density_tile(own[0:5, lanes(i)])
         return 0
 
     lax.fori_loop(0, nb, own_tile, 0, unroll=4)
     b_ref[nb] = jnp.zeros((KF, BLK), bf16)
-    acc[...] = jnp.zeros_like(acc)
+    acc[0:nb] = start[...]
+    acc[nb] = jnp.zeros((8, BLK), f32)
 
     def work(at, size):
         for g in range(size):
             code = lst[at + g]
             e = jnp.dot(a_ref[code & 255], b_ref[code >> 8], preferred_element_type=f32)
-            acc[code >> 8] += jnp.exp2(e).reshape(BLK // 8, 8, BLK).sum(0)
+            acc[code >> 8] += column_sums(e)
 
     fetch.wait()
-    for_groups(lst, work)
+    for_groups(lst, work, 2 * nb)
     d = acc[0:nb].sum(1) * (1.0 / (NP * BLK))
     den[...] = d
     term[...] = jnp.exp2(jnp.log2(d) * (-1.0 / 3.0))
 
 
-def density(own, lo, hi, a_own, lst):
+def density(own, lo, hi, a_own, start, lst):
     nb = a_own.shape[0]
     return pl.pallas_call(
         density_kernel,
@@ -329,7 +355,7 @@
             jax.ShapeDtypeStruct((nb, BLK), f32),
             jax.ShapeDtypeStruct((2 * nb, BLK, KF), bf16),
         ],
-        in_specs=[VM, VM, VM, VM, AN],
+        in_specs=[VM, VM, VM, VM, VM, AN],
         out_specs=[VM] * 3,
         scratch_shapes=[
             pltpu.VMEM((nb + 1, KF, BLK), bf16),
@@ -340,7 +366,7 @@
         compiler_params=pltpu.CompilerParams(vmem_limit_bytes=16 << 20),
         cost_estimate=pl.CostEstimate(flops=12 * nb * NP * BLK * BLK, bytes_accessed=8 << 20, transcendentals=nb * NP * BLK * BLK),
         name="density",
-    )(own, lo, hi, a_own, lst)
+    )(own, lo, hi, a_own, start, lst)
 
 
 def force_kernel(own, lo, hi, a_ref, town, tlo, thi, listed, out, b_ref, v_ref, acc, lst, sem):
@@ -399,7 +425,7 @@
                 acc[code >> 8] += jnp.dot(v_ref[code & 255], weights.pop(g), preferred_element_type=f32)
 
     fetch.wait()
-    for_groups(lst, work)
+    for_groups(lst, work, 0)
 
     def finish(i, _):
         a = acc[i]
@@ -445,8 +471,8 @@
     )
     lo = lax.ppermute(tail, "slab", up)
     hi = lax.ppermute(head, "slab", down)
-    grid, rim, a_own = deposit_own(own)
-    den, term, a = density(own, lo, hi, a_own, lst)
+    grid, rim, a_own, start = deposit_own(own)
+    den, term, a = density(own, lo, hi, a_own, start, lst)
     tlo = lax.ppermute(term[hb:], "slab", up)
     thi = lax.ppermute(term[:hb], "slab", down)
     grid, rim, edge_row = deposit_in(lo, grid, rim, term)

time: 63.1 us -> 62.8 us (level)
  the two profiles are of different devices: /device:TPU:16 before, /device:TPU:24 now
where the time goes in v5:
time: 62.8 us; the launch traced here: 62.3 us
  Pallas kernels  31.2 us (50%)
  starting transfers between devices  25.4 us (40%)
  local copies, waits for them, and re-layouts  2.56 us (4%)
  waiting for transfers between devices  2.34 us (4%)
  between operations  0.75 us (1%)
    ppermute x1, starting transfers between devices, on_device(): hi = lax.ppermute(head, 'slab', down)  13.3 us
    pallas_call x1, Pallas kernels, force(): pl.pallas_call(force_kernel, out_shape=jax.ShapeDtypeStruct((3, nb * BLK)...  11.9 us
    pallas_call x1, Pallas kernels, deposit_own(): pl.pallas_call(deposit_own_kernel, out_shape=[jax.ShapeDtypeStruct((XP, M...  7.35 us
    ppermute x1, starting transfers between devices, on_device(): thi = lax.ppermute(term[:hb], 'slab', down)  6.13 us
    pallas_call x1, Pallas kernels, density(): pl.pallas_call(density_kernel, out_shape=[jax.ShapeDtypeStruct((nb, BLK),...  5.95 us
    pallas_call x1, Pallas kernels, deposit_in(): pl.pallas_call(deposit_in_kernel, out_shape=[jax.ShapeDtypeStruct((XP, MY...  3.41 us
    pallas_call x1, Pallas kernels, pack(): pl.pallas_call(pack_kernel, out_shape=[jax.ShapeDtypeStruct((10, n), f32)...  2.6 us
    ppermute x1, starting transfers between devices, on_device(): rows = lax.ppermute(rim[:XP], 'col', right)  2.16 us
  transfers between devices with their start and end apart: 5, of which 2 were waited for; matrix products, arithmetic and copies ran while one was open for 0% of the time, Pallas kernels for 36%

profile of v5, /device:TPU:24, one launch (start us, length us, event | category | flops | bytes accessed | tf_op | source)
XLA Modules:
  0.0 62.3 jit_solution(2217507362343584445)
XLA Ops:
  0.6 2.6 %pack.1 = (f32[10,8192]{1,0:T(8,128)}, f32[10,4096]{1,0:T(8,128)}, f32[5,4096]{1,0:T(8,128)}, s32[617]{0:T(1024)}) custom-call(f32[3,8192]{1,0:T(4,128)} %pos.1, f32[1,8192]{1,0:T(1,128)} %bitcast.7, f32[1,8192]{1,0:T(1,128)} %bitcast.8, s32[1,8192]{1,0:T(1,128)} %bitcast.9, s32[1,8192]{1,0:T(1,128)} %bitcast.10, f32[3,8192]{1,0:T(4,128)} %frac.1, ...), custom_call_target="tpu_custom_call" | custom-call | tf_op jit(solution)/shard_map/pack/pallas_call | solution.py:81
  3.2 13.3 %collective-permute-start.1 = (f32[5,4096]{1,0:T(8,128)}, f32[5,4096]{1,0:T(8,128)S(1)}, u32[]{:S(2)}, u32[]{:S(2)}) collective-permute-start(f32[5,4096]{1,0:T(8,128)} %get-tuple-element.21), channel_id=1, source_target_pairs={{8,0},{16,8},{24,16},{32,24},{40,32},{48,40},{56,48},{64,56},{72,6... | collective-permute-start | bytes 245768 | tf_op jit(solution)/shard_map/ppermute | solution.py:473
  16.6 1.9 %collective-permute-start = (f32[10,4096]{1,0:T(8,128)}, f32[10,4096]{1,0:T(8,128)S(1)}, u32[]{:S(2)}, u32[]{:S(2)}) collective-permute-start(f32[10,4096]{1,0:T(8,128)} %get-tuple-element.20), channel_id=1, source_target_pairs={{0,8},{8,16},{16,24},{24,32},{32,40},{40,48},{48,56},{56,64},{64,7... | collective-permute-start | bytes 491528 | tf_op jit(solution)/shard_map/ppermute | solution.py:472
  18.5 0.0 copy-start
  18.5 1.0 %copy-done = f32[10,8192]{1,0:T(8,128)S(1)} copy-done((f32[10,8192]{1,0:T(8,128)S(1)}, f32[10,8192]{1,0:T(8,128)}, u32[]{:S(2)}) %copy-start) | copy-done | bytes 327704
  19.5 0.0 copy-start.2
  19.5 7.4 %deposit_own.1 = (f32[2,128,1024]{2,1,0:T(8,128)S(1)}, f32[8,1024]{1,0:T(8,128)S(1)}, bf16[64,128,48]{2,1,0:T(8,128)(2,1)S(1)}, f32[64,8,128]{2,1,0:T(8,128)S(1)}) custom-call(f32[10,8192]{1,0:T(8,128)S(1)} %copy-done), custom_call_target="tpu_custom_call" | custom-call | flops 4294967296 | bytes 4194304 | tf_op jit(solution)/shard_map/deposit_own/pallas_call | solution.py:252
  26.9 0.0 collective-permute-done.1.hi
  26.9 1.2 %collective-permute-done.lo.st = f32[10,4096]{1,0:T(8,128)S(1)} collective-permute-done((f32[10,4096]{1,0:T(8,128)}, f32[10,4096]{1,0:T(8,128)S(1)}, u32[]{:S(2)}, u32[]{:S(2)}) %collective-permute-start) | collective-permute-done | bytes 163872 | tf_op jit(solution)/shard_map/ppermute | solution.py:472
  28.1 0.0 copy-done.2
  28.1 0.0 copy-start.1
  28.1 6.0 %density.1 = (f32[64,128]{1,0:T(8,128)}, f32[64,128]{1,0:T(8,128)S(1)}, bf16[128,128,48]{2,1,0:T(8,128)(2,1)S(1)}) custom-call(f32[10,8192]{1,0:T(8,128)S(1)} %copy-done, f32[10,4096]{1,0:T(8,128)S(1)} %collective-permute-done.lo.st, f32[5,4096]{1,0:T(8,128)S(1)} %collective-permute-done.1.hi, bf16[64,128,48]{2,1,0:T(8,128)(2,1)S(1)} %get-tuple-element.22.a_own, ...), custom_call_target="tpu_custom_call" | custom-call | flops 113246208 | bytes 8388608 | tf_op jit(solution)/shard_map/density/pallas_call | solution.py:351
  34.0 6.1 %collective-permute-start.4 = (f32[32,128]{1,0:T(8,128)S(1)}, f32[32,128]{1,0:T(8,128)S(1)}, u32[]{:S(2)}, u32[]{:S(2)}) collective-permute-start(f32[32,128]{1,0:T(8,128)S(1)} %get-tuple-element.35), channel_id=1, source_target_pairs={{8,0},{16,8},{24,16},{32,24},{40,32},{48,40},{56,48},{64,56},{72,6... | collective-permute-start | bytes 49160 | tf_op jit(solution)/shard_map/ppermute | solution.py:477
  40.2 1.9 %collective-permute-start.3 = (f32[32,128]{1,0:T(8,128)S(1)}, f32[32,128]{1,0:T(8,128)S(1)}, u32[]{:S(2)}, u32[]{:S(2)}) collective-permute-start(f32[32,128]{1,0:T(8,128)S(1)} %get-tuple-element.36), channel_id=1, source_target_pairs={{0,8},{8,16},{16,24},{24,32},{32,40},{40,48},{48,56},{56,64},{64,7... | collective-permute-start | bytes 49160 | tf_op jit(solution)/shard_map/ppermute | solution.py:476
  42.1 3.4 %deposit_in.1 = (f32[2,128,1024]{2,1,0:T(8,128)}, f32[8,1024]{1,0:T(8,128)S(1)}, f32[2,1,1024]{2,1,0:T(1,128)S(1)}) custom-call(f32[10,4096]{1,0:T(8,128)S(1)} %collective-permute-done.lo.st, f32[2,128,1024]{2,1,0:T(8,128)S(1)} %get-tuple-element.26.g_in, f32[8,1024]{1,0:T(8,128)S(1)} %get-tuple-element.27.r_in, f32[64,128]{1,0:T(8,128)S(1)} %get-tuple-element.28.after.town), custom_call_target="tpu_custom_call" | custom-call | flops 1073741824 | bytes 4194304 | tf_op jit(solution)/shard_map/deposit_in/pallas_call | solution.py:286
  45.5 2.2 %collective-permute-start.2 = (f32[2,1024]{1,0:T(2,128)S(1)}, f32[2,1024]{1,0:T(2,128)S(1)}, u32[]{:S(2)}, u32[]{:S(2)}) collective-permute-start(f32[2,1024]{1,0:T(2,128)S(1)} %slice.9), channel_id=1, source_target_pairs={{0,1},{1,2},{2,3},{3,4},{4,5},{5,6},{6,7},{7,0},{8,9},{9,10},{10,1... | collective-permute-start | bytes 24584 | tf_op jit(solution)/shard_map/ppermute | solution.py:479
  47.7 0.0 collective-permute-done.4.thi
  47.7 1.2 %collective-permute-done.3.tlo = f32[32,128]{1,0:T(8,128)S(1)} collective-permute-done((f32[32,128]{1,0:T(8,128)S(1)}, f32[32,128]{1,0:T(8,128)S(1)}, u32[]{:S(2)}, u32[]{:S(2)}) %collective-permute-start.3) | collective-permute-done | bytes 16416 | tf_op jit(solution)/shard_map/ppermute | solution.py:476
  48.9 0.0 copy-done.1
  48.9 11.9 %force.1 = f32[3,8192]{1,0:T(4,128)} custom-call(f32[10,8192]{1,0:T(8,128)S(1)} %copy-done.1, f32[10,4096]{1,0:T(8,128)S(1)} %collective-permute-done.lo.st, f32[5,4096]{1,0:T(8,128)S(1)} %collective-permute-done.1.hi, bf16[128,128,48]{2,1,0:T(8,128)(2,1)S(1)} %get-tuple-element.30.a_ref, f32[64,128]{1,0:T(8,128)S(1)} %get-tuple-element.28.after.town, ...), custom_call_target="tpu_custom_call" | custom-call | flops 226492416 | bytes 8388608 | tf_op jit(solution)/shard_map/force/pallas_call | solution.py:444
  60.8 0.0 collective-permute-done.2
  60.8 1.5 %dynamic_update_slice.3 = f32[2,128,1024]{2,1,0:T(8,128)} dynamic-update-slice(f32[2,128,1024]{2,1,0:T(8,128)} %get-tuple-element.32, f32[2,1,1024]{2,1,0:T(1,128)S(1)} %reshape_add_fusion, s32[]{:T(128)} %constant.0.clone.1, s32[]{:T(128)} %constant.0.clone.1, s32[]{:T(128)} %constant.0.clone.1) | dynamic-update-slice | bytes 16388 | tf_op jit(solution)/shard_map/dynamic_update_slice | solution.py:482
  (3 shorter events, 0.0 us)
Async XLA Ops:
  3.2 23.6 %collective-permute-start.1 = (f32[5,4096]{1,0:T(8,128)}, f32[5,4096]{1,0:T(8,128)S(1)}, u32[]{:S(2)}, u32[]{:S(2)}) collective-permute-start(f32[5,4096]{1,0:T(8,128)} %get-tuple-element.21), channel_id=1, source_target_pairs={{8,0},{16,8},{24,16},{32,24},{40,32},{48,40},{56,48},{64,56},{72,6... | collective-permute-start | bytes 245768 | tf_op jit(solution)/shard_map/ppermute | solution.py:473
  16.6 11.5 %collective-permute-start = (f32[10,4096]{1,0:T(8,128)}, f32[10,4096]{1,0:T(8,128)S(1)}, u32[]{:S(2)}, u32[]{:S(2)}) collective-permute-start(f32[10,4096]{1,0:T(8,128)} %get-tuple-element.20), channel_id=1, source_target_pairs={{0,8},{8,16},{16,24},{24,32},{32,40},{40,48},{48,56},{56,64},{64,7... | collective-permute-start | bytes 491528 | tf_op jit(solution)/shard_map/ppermute | solution.py:472
  18.5 1.0 %copy-start = (f32[10,8192]{1,0:T(8,128)S(1)}, f32[10,8192]{1,0:T(8,128)}, u32[]{:S(2)}) copy-start(f32[10,8192]{1,0:T(8,128)} %get-tuple-element.19.st.own) | copy-start | bytes 983044
  19.5 8.5 %copy-start.2 = (s32[617]{0:T(1024)S(1)}, s32[617]{0:T(1024)}, u32[]{:S(2)}) copy-start(s32[617]{0:T(1024)} %get-tuple-element.24.listed) | copy-start | bytes 7408
  28.1 20.8 %copy-start.1 = (f32[10,8192]{1,0:T(8,128)S(1)}, f32[10,8192]{1,0:T(8,128)}, u32[]{:S(2)}) copy-start(f32[10,8192]{1,0:T(8,128)} %get-tuple-element.19.st.own) | copy-start | bytes 983044
  34.0 13.6 %collective-permute-start.4 = (f32[32,128]{1,0:T(8,128)S(1)}, f32[32,128]{1,0:T(8,128)S(1)}, u32[]{:S(2)}, u32[]{:S(2)}) collective-permute-start(f32[32,128]{1,0:T(8,128)S(1)} %get-tuple-element.35), channel_id=1, source_target_pairs={{8,0},{16,8},{24,16},{32,24},{40,32},{48,40},{56,48},{64,56},{72,6... | collective-permute-start | bytes 49160 | tf_op jit(solution)/shard_map/ppermute | solution.py:477
  40.2 8.7 %collective-permute-start.3 = (f32[32,128]{1,0:T(8,128)S(1)}, f32[32,128]{1,0:T(8,128)S(1)}, u32[]{:S(2)}, u32[]{:S(2)}) collective-permute-start(f32[32,128]{1,0:T(8,128)S(1)} %get-tuple-element.36), channel_id=1, source_target_pairs={{0,8},{8,16},{16,24},{24,32},{32,40},{40,48},{48,56},{56,64},{64,7... | collective-permute-start | bytes 49160 | tf_op jit(solution)/shard_map/ppermute | solution.py:476
  45.5 15.2 %collective-permute-start.2 = (f32[2,1024]{1,0:T(2,128)S(1)}, f32[2,1024]{1,0:T(2,128)S(1)}, u32[]{:S(2)}, u32[]{:S(2)}) collective-permute-start(f32[2,1024]{1,0:T(2,128)S(1)} %slice.9), channel_id=1, source_target_pairs={{0,1},{1,2},{2,3},{3,4},{4,5},{5,6},{6,7},{7,0},{8,9},{9,10},{10,1... | collective-permute-start | bytes 24584 | tf_op jit(solution)/shard_map/ppermute | solution.py:479

commit v6 on v5

--- a/solution.py
+++ b/solution.py
@@ -35,8 +35,8 @@
     return pl.ds(pl.multiple_of(i * width, BLK), width)
 
 
-def pack_kernel(pos, mass, smooth, cy, cz, frac, pairs, counts, own, tail, head, lst, spairs, scounts, vpos, vmass, vsmooth, vcy, vcz, vfrac, sems):
-    half = own.shape[1] // 2
+def pack_kernel(pos, mass, smooth, cy, cz, frac, pairs, counts, own_out, tail, head_out, lst, spairs, scounts, vpos, vmass, vsmooth, vcy, vcz, vfrac, own, head, sems):
+    half = tail.shape[1]
     moves = (
         (pos, vpos),
         (mass, vmass),
@@ -52,6 +52,20 @@
         copy.start()
     for copy in copies[-2:] + copies[:-2]:
         copy.wait()
+    own[0:3] = vpos[...]
+    own[3:4] = vmass[...]
+    own[4:5] = vsmooth[...]
+    own[5:6] = vcy[...].astype(f32)
+    own[6:7] = vcz[...].astype(f32)
+    own[7:10] = vfrac[...]
+    head[...] = own[0:5, :half]
+    sends = [
+        pltpu.make_async_copy(own.at[:, pl.ds(half, half)], tail, sems.at[8]),
+        pltpu.make_async_copy(head, head_out, sems.at[9]),
+        pltpu.make_async_copy(own, own_out, sems.at[10]),
+    ]
+    for copy in sends:
+        copy.start()
     nb = counts.shape[1]
     hb = nb // 2
     for b in range(hb):
@@ -65,14 +79,8 @@
     for k in range(REST):
         lst[at + k] = i32(nb * 256)
     lst[lst.shape[0] - 1] = at
-    own[0:3] = vpos[...]
-    own[3:4] = vmass[...]
-    own[4:5] = vsmooth[...]
-    own[5:6] = vcy[...].astype(f32)
-    own[6:7] = vcz[...].astype(f32)
-    own[7:10] = vfrac[...]
-    tail[...] = own[:, half:]
-    head[...] = own[0:5, :half]
+    for copy in sends:
+        copy.wait()
 
 
 def pack(positions, mass, smooth, cell_y, cell_z, cic_frac, pairs, counts):
@@ -87,7 +95,7 @@
             jax.ShapeDtypeStruct((nb * NP + NP + 2 * REST,), i32),
         ],
         in_specs=[HB] * 8,
-        out_specs=[VM] * 3 + [SM],
+        out_specs=[HB] * 3 + [SM],
         scratch_shapes=[
             pltpu.SMEM((NP, nb), i32),
             pltpu.SMEM((1, nb), i32),
@@ -97,7 +105,9 @@
             pltpu.VMEM((1, n), i32),
             pltpu.VMEM((1, n), i32),
             pltpu.VMEM((3, n), f32),
-            pltpu.SemaphoreType.DMA((8,)),
+            pltpu.VMEM((10, n), f32),
+            pltpu.VMEM((5, n // 2), f32),
+            pltpu.SemaphoreType.DMA((11,)),
         ],
         name="pack",
     )(positions, mass[None], smooth[None], cell_y[None], cell_z[None], cic_frac, pairs, counts[None])

time: 62.8 us -> 62.8 us (level)
  the two profiles are of different devices: /device:TPU:24 before, /device:TPU:8 now
where the time goes in v6:
time: 62.8 us; the launch traced here: 62.4 us
  Pallas kernels  31.3 us (50%)
  starting transfers between devices  26.3 us (42%)
  local copies, waits for them, and re-layouts  2.56 us (4%)
  waiting for transfers between devices  1.43 us (2%)
  between operations  0.75 us (1%)
    ppermute x1, starting transfers between devices, on_device(): hi = lax.ppermute(head, 'slab', down)  13.3 us
    pallas_call x1, Pallas kernels, force(): pl.pallas_call(force_kernel, out_shape=jax.ShapeDtypeStruct((3, nb * BLK)...  11.9 us
    pallas_call x1, Pallas kernels, deposit_own(): pl.pallas_call(deposit_own_kernel, out_shape=[jax.ShapeDtypeStruct((XP, M...  7.37 us
    ppermute x1, starting transfers between devices, on_device(): thi = lax.ppermute(term[:hb], 'slab', down)  6.12 us
    pallas_call x1, Pallas kernels, density(): pl.pallas_call(density_kernel, out_shape=[jax.ShapeDtypeStruct((nb, BLK),...  5.94 us
    pallas_call x1, Pallas kernels, deposit_in(): pl.pallas_call(deposit_in_kernel, out_shape=[jax.ShapeDtypeStruct((XP, MY...  3.41 us
    ppermute x1, starting transfers between devices, on_device(): rows = lax.ppermute(rim[:XP], 'col', right)  3.05 us
    pallas_call x1, Pallas kernels, pack(): pl.pallas_call(pack_kernel, out_shape=[jax.ShapeDtypeStruct((10, n), f32)...  2.74 us
  transfers between devices with their start and end apart: 5, of which 2 were waited for; matrix products, arithmetic and copies ran while one was open for 0% of the time, Pallas kernels for 36%

profile of v6, /device:TPU:8, one launch (start us, length us, event | category | flops | bytes accessed | tf_op | source)
XLA Modules:
  0.0 62.4 jit_solution(7980808755500128632)
XLA Ops:
  0.6 2.7 %pack.1 = (f32[10,8192]{1,0:T(8,128)}, f32[10,4096]{1,0:T(8,128)}, f32[5,4096]{1,0:T(8,128)}, s32[617]{0:T(1024)}) custom-call(f32[3,8192]{1,0:T(4,128)} %pos.1, f32[1,8192]{1,0:T(1,128)} %bitcast.7, f32[1,8192]{1,0:T(1,128)} %bitcast.8, s32[1,8192]{1,0:T(1,128)} %bitcast.9, s32[1,8192]{1,0:T(1,128)} %bitcast.10, f32[3,8192]{1,0:T(4,128)} %frac.1, ...), custom_call_target="tpu_custom_call" | custom-call | tf_op jit(solution)/shard_map/pack/pallas_call | solution.py:89
  3.4 13.3 %collective-permute-start.1 = (f32[5,4096]{1,0:T(8,128)}, f32[5,4096]{1,0:T(8,128)S(1)}, u32[]{:S(2)}, u32[]{:S(2)}) collective-permute-start(f32[5,4096]{1,0:T(8,128)} %get-tuple-element.21), channel_id=1, source_target_pairs={{8,0},{16,8},{24,16},{32,24},{40,32},{48,40},{56,48},{64,56},{72,6... | collective-permute-start | bytes 245768 | tf_op jit(solution)/shard_map/ppermute | solution.py:483
  16.7 1.9 %collective-permute-start = (f32[10,4096]{1,0:T(8,128)}, f32[10,4096]{1,0:T(8,128)S(1)}, u32[]{:S(2)}, u32[]{:S(2)}) collective-permute-start(f32[10,4096]{1,0:T(8,128)} %get-tuple-element.20), channel_id=1, source_target_pairs={{0,8},{8,16},{16,24},{24,32},{32,40},{40,48},{48,56},{56,64},{64,7... | collective-permute-start | bytes 491528 | tf_op jit(solution)/shard_map/ppermute | solution.py:482
  18.6 0.0 copy-start
  18.6 1.0 %copy-done = f32[10,8192]{1,0:T(8,128)S(1)} copy-done((f32[10,8192]{1,0:T(8,128)S(1)}, f32[10,8192]{1,0:T(8,128)}, u32[]{:S(2)}) %copy-start) | copy-done | bytes 327704
  19.7 0.0 copy-start.2
  19.7 7.4 %deposit_own.1 = (f32[2,128,1024]{2,1,0:T(8,128)S(1)}, f32[8,1024]{1,0:T(8,128)S(1)}, bf16[64,128,48]{2,1,0:T(8,128)(2,1)S(1)}, f32[64,8,128]{2,1,0:T(8,128)S(1)}) custom-call(f32[10,8192]{1,0:T(8,128)S(1)} %copy-done), custom_call_target="tpu_custom_call" | custom-call | flops 4294967296 | bytes 4194304 | tf_op jit(solution)/shard_map/deposit_own/pallas_call | solution.py:262
  27.0 0.0 collective-permute-done.1.hi
  27.1 1.2 %collective-permute-done.lo.st = f32[10,4096]{1,0:T(8,128)S(1)} collective-permute-done((f32[10,4096]{1,0:T(8,128)}, f32[10,4096]{1,0:T(8,128)S(1)}, u32[]{:S(2)}, u32[]{:S(2)}) %collective-permute-start) | collective-permute-done | bytes 163872 | tf_op jit(solution)/shard_map/ppermute | solution.py:482
  28.2 0.0 copy-done.2
  28.2 0.0 copy-start.1
  28.2 5.9 %density.1 = (f32[64,128]{1,0:T(8,128)}, f32[64,128]{1,0:T(8,128)S(1)}, bf16[128,128,48]{2,1,0:T(8,128)(2,1)S(1)}) custom-call(f32[10,8192]{1,0:T(8,128)S(1)} %copy-done, f32[10,4096]{1,0:T(8,128)S(1)} %collective-permute-done.lo.st, f32[5,4096]{1,0:T(8,128)S(1)} %collective-permute-done.1.hi, bf16[64,128,48]{2,1,0:T(8,128)(2,1)S(1)} %get-tuple-element.22.a_own, ...), custom_call_target="tpu_custom_call" | custom-call | flops 113246208 | bytes 8388608 | tf_op jit(solution)/shard_map/density/pallas_call | solution.py:361
  34.2 6.1 %collective-permute-start.4 = (f32[32,128]{1,0:T(8,128)S(1)}, f32[32,128]{1,0:T(8,128)S(1)}, u32[]{:S(2)}, u32[]{:S(2)}) collective-permute-start(f32[32,128]{1,0:T(8,128)S(1)} %get-tuple-element.35), channel_id=1, source_target_pairs={{8,0},{16,8},{24,16},{32,24},{40,32},{48,40},{56,48},{64,56},{72,6... | collective-permute-start | bytes 49160 | tf_op jit(solution)/shard_map/ppermute | solution.py:487
  40.3 1.9 %collective-permute-start.3 = (f32[32,128]{1,0:T(8,128)S(1)}, f32[32,128]{1,0:T(8,128)S(1)}, u32[]{:S(2)}, u32[]{:S(2)}) collective-permute-start(f32[32,128]{1,0:T(8,128)S(1)} %get-tuple-element.36), channel_id=1, source_target_pairs={{0,8},{8,16},{16,24},{24,32},{32,40},{40,48},{48,56},{56,64},{64,7... | collective-permute-start | bytes 49160 | tf_op jit(solution)/shard_map/ppermute | solution.py:486
  42.2 3.4 %deposit_in.1 = (f32[2,128,1024]{2,1,0:T(8,128)}, f32[8,1024]{1,0:T(8,128)S(1)}, f32[2,1,1024]{2,1,0:T(1,128)S(1)}) custom-call(f32[10,4096]{1,0:T(8,128)S(1)} %collective-permute-done.lo.st, f32[2,128,1024]{2,1,0:T(8,128)S(1)} %get-tuple-element.26.g_in, f32[8,1024]{1,0:T(8,128)S(1)} %get-tuple-element.27.r_in, f32[64,128]{1,0:T(8,128)S(1)} %get-tuple-element.28.after.town), custom_call_target="tpu_custom_call" | custom-call | flops 1073741824 | bytes 4194304 | tf_op jit(solution)/shard_map/deposit_in/pallas_call | solution.py:296
  45.6 3.0 %collective-permute-start.2 = (f32[2,1024]{1,0:T(2,128)S(1)}, f32[2,1024]{1,0:T(2,128)S(1)}, u32[]{:S(2)}, u32[]{:S(2)}) collective-permute-start(f32[2,1024]{1,0:T(2,128)S(1)} %slice.9), channel_id=1, source_target_pairs={{0,1},{1,2},{2,3},{3,4},{4,5},{5,6},{6,7},{7,0},{8,9},{9,10},{10,1... | collective-permute-start | bytes 24584 | tf_op jit(solution)/shard_map/ppermute | solution.py:489
  48.7 0.0 collective-permute-done.4.thi
  48.7 0.3 collective-permute-done.3.tlo
  49.0 0.0 copy-done.1
  49.0 11.9 %force.1 = f32[3,8192]{1,0:T(4,128)} custom-call(f32[10,8192]{1,0:T(8,128)S(1)} %copy-done.1, f32[10,4096]{1,0:T(8,128)S(1)} %collective-permute-done.lo.st, f32[5,4096]{1,0:T(8,128)S(1)} %collective-permute-done.1.hi, bf16[128,128,48]{2,1,0:T(8,128)(2,1)S(1)} %get-tuple-element.30.a_ref, f32[64,128]{1,0:T(8,128)S(1)} %get-tuple-element.28.after.town, ...), custom_call_target="tpu_custom_call" | custom-call | flops 226492416 | bytes 8388608 | tf_op jit(solution)/shard_map/force/pallas_call | solution.py:454
  60.9 0.0 collective-permute-done.2
  60.9 1.5 %dynamic_update_slice.3 = f32[2,128,1024]{2,1,0:T(8,128)} dynamic-update-slice(f32[2,128,1024]{2,1,0:T(8,128)} %get-tuple-element.32, f32[2,1,1024]{2,1,0:T(1,128)S(1)} %reshape_add_fusion, s32[]{:T(128)} %constant.0.clone.1, s32[]{:T(128)} %constant.0.clone.1, s32[]{:T(128)} %constant.0.clone.1) | dynamic-update-slice | bytes 16388 | tf_op jit(solution)/shard_map/dynamic_update_slice | solution.py:492
  (3 shorter events, 0.0 us)
Async XLA Ops:
  3.4 23.7 %collective-permute-start.1 = (f32[5,4096]{1,0:T(8,128)}, f32[5,4096]{1,0:T(8,128)S(1)}, u32[]{:S(2)}, u32[]{:S(2)}) collective-permute-start(f32[5,4096]{1,0:T(8,128)} %get-tuple-element.21), channel_id=1, source_target_pairs={{8,0},{16,8},{24,16},{32,24},{40,32},{48,40},{56,48},{64,56},{72,6... | collective-permute-start | bytes 245768 | tf_op jit(solution)/shard_map/ppermute | solution.py:483
  16.7 11.5 %collective-permute-start = (f32[10,4096]{1,0:T(8,128)}, f32[10,4096]{1,0:T(8,128)S(1)}, u32[]{:S(2)}, u32[]{:S(2)}) collective-permute-start(f32[10,4096]{1,0:T(8,128)} %get-tuple-element.20), channel_id=1, source_target_pairs={{0,8},{8,16},{16,24},{24,32},{32,40},{40,48},{48,56},{56,64},{64,7... | collective-permute-start | bytes 491528 | tf_op jit(solution)/shard_map/ppermute | solution.py:482
  18.6 1.0 %copy-start = (f32[10,8192]{1,0:T(8,128)S(1)}, f32[10,8192]{1,0:T(8,128)}, u32[]{:S(2)}) copy-start(f32[10,8192]{1,0:T(8,128)} %get-tuple-element.19.st.own) | copy-start | bytes 983044
  19.7 8.5 %copy-start.2 = (s32[617]{0:T(1024)S(1)}, s32[617]{0:T(1024)}, u32[]{:S(2)}) copy-start(s32[617]{0:T(1024)} %get-tuple-element.24.listed) | copy-start | bytes 7408
  28.2 20.8 %copy-start.1 = (f32[10,8192]{1,0:T(8,128)S(1)}, f32[10,8192]{1,0:T(8,128)}, u32[]{:S(2)}) copy-start(f32[10,8192]{1,0:T(8,128)} %get-tuple-element.19.st.own) | copy-start | bytes 983044
  34.2 14.5 %collective-permute-start.4 = (f32[32,128]{1,0:T(8,128)S(1)}, f32[32,128]{1,0:T(8,128)S(1)}, u32[]{:S(2)}, u32[]{:S(2)}) collective-permute-start(f32[32,128]{1,0:T(8,128)S(1)} %get-tuple-element.35), channel_id=1, source_target_pairs={{8,0},{16,8},{24,16},{32,24},{40,32},{48,40},{56,48},{64,56},{72,6... | collective-permute-start | bytes 49160 | tf_op jit(solution)/shard_map/ppermute | solution.py:487
  40.3 8.7 %collective-permute-start.3 = (f32[32,128]{1,0:T(8,128)S(1)}, f32[32,128]{1,0:T(8,128)S(1)}, u32[]{:S(2)}, u32[]{:S(2)}) collective-permute-start(f32[32,128]{1,0:T(8,128)S(1)} %get-tuple-element.36), channel_id=1, source_target_pairs={{0,8},{8,16},{16,24},{24,32},{32,40},{40,48},{48,56},{56,64},{64,7... | collective-permute-start | bytes 49160 | tf_op jit(solution)/shard_map/ppermute | solution.py:486
  45.6 15.2 %collective-permute-start.2 = (f32[2,1024]{1,0:T(2,128)S(1)}, f32[2,1024]{1,0:T(2,128)S(1)}, u32[]{:S(2)}, u32[]{:S(2)}) collective-permute-start(f32[2,1024]{1,0:T(2,128)S(1)} %slice.9), channel_id=1, source_target_pairs={{0,1},{1,2},{2,3},{3,4},{4,5},{5,6},{6,7},{7,0},{8,9},{9,10},{10,1... | collective-permute-start | bytes 24584 | tf_op jit(solution)/shard_map/ppermute | solution.py:489
